TPU v7x, 32 devices: a whole 2x2x4 slice. The times are simulated.
32 devices in a mesh: dp: 16 (over z, y, core), seq: 2 (over x).
Axes of the slice: x: 2, y: 2, z: 4, core: 2. Of those that a mesh axis runs over, the one named last changes fastest.
Arguments:
- tokens: bfloat16 [32, 1024, 1152], P('dp', 'seq'), may hold values from -6 to 6
- cotangent: bfloat16 [32, 1024, 1152], P('dp', 'seq'), may hold values from -6 to 6
- lengths: int32 [32, 10], P('dp'), may hold values from 0 to 1024, as said below
- adapter_ids: int32 [32, 10], P('dp'), may hold values from 0 to 7
- w_query: bfloat16 [1152, 1152], P('dp', 'seq'), may hold values from -0.1875 to 0.1875
- w_key: bfloat16 [1152, 1152], P('dp', 'seq'), may hold values from -0.1875 to 0.1875
- w_value: bfloat16 [1152, 1152], P('dp', 'seq'), may hold values from -0.1875 to 0.1875
- w_out: bfloat16 [1152, 1152], P('dp', 'seq'), may hold values from -2 to 2
- w_up: bfloat16 [1152, 4304], P('dp', 'seq'), may hold values from -0.1875 to 0.1875
- w_down: bfloat16 [4304, 1152], P('seq', 'dp'), may hold values from -0.09375 to 0.09375
- b_query: bfloat16 [1152], P('seq'), may hold values from -3 to 3
- b_value: bfloat16 [1152], P('seq'), may hold values from -0.29882812 to 0.29882812
- b_out: bfloat16 [1152], P('seq'), may hold values from -1.796875 to 1.796875
- b_up: bfloat16 [4304], P('seq'), may hold values from -3 to 3
- b_down: bfloat16 [1152], P('seq'), may hold values from -1.796875 to 1.796875
- gain_one: bfloat16 [1152], P('seq'), may hold values from 0.5 to 1.5
- shift_one: bfloat16 [1152], P('seq'), may hold values from -1.796875 to 1.796875
- gain_two: bfloat16 [1152], P('seq'), may hold values from 0.5 to 1.5
- shift_two: bfloat16 [1152], P('seq'), may hold values from -1.796875 to 1.796875
- qkv_a: bfloat16 [3, 8, 1152, 16], P(None, 'seq'), may hold values from -0.1875 to 0.1875
- out_a: bfloat16 [8, 1152, 16], P('seq'), may hold values from -2 to 2
- attn_b: bfloat16 [4, 8, 16, 1152], P(None, 'seq'), may hold values from -1.5 to 1.5
- up_a: bfloat16 [8, 1152, 16], P('seq'), may hold values from -0.1875 to 0.1875
- up_b: bfloat16 [8, 16, 4304], P('seq'), may hold values from -1.5 to 1.5
- down_a: bfloat16 [8, 4304, 16], P('seq'), may hold values from -0.09375 to 0.09375
- down_b: bfloat16 [8, 16, 1152], P('seq'), may hold values from -1.5 to 1.5
Outputs:
- mixed: bfloat16 [32, 1024, 1152], P('dp', 'seq')
- input_grad: float32 [32, 1024, 1152], P('dp', 'seq')
- grad_qkv_a: float32 [3, 8, 1152, 16], P(None, 'seq')
- grad_out_a: float32 [8, 1152, 16], P('seq')
- grad_attn_b: float32 [4, 8, 16, 1152], P(None, 'seq')
- grad_up_a: float32 [8, 1152, 16], P('seq')
- grad_up_b: float32 [8, 16, 4304], P('seq')
- grad_down_a: float32 [8, 4304, 16], P('seq')
- grad_down_b: float32 [8, 16, 1152], P('seq')
Inputs may be any that keep to these rules, and one draw needn't show every extreme that they name: `lengths`: each row lists the patch counts of its pictures in order, each 100 to 1024, then zeros; the counts sum to at most 1024 and the rest of the row is padding. In each aligned group of 2 rows one row holds a single picture of 1024 patches. `adapter_ids`: slots after a row's last picture are unused.
All inputs are finite; a program needn't handle non-finite values.
Results may differ from a plain program's by a relative error of at most 0.019.
Values may be sent and summed in bfloat16 or wider, within the bound.
A program may use at most 320 MiB of HBM per device.

v0:
```python
from functools import partial

import jax
import jax.numpy as jnp
from jax import lax
from jax.experimental import pallas as pl
from jax.experimental.pallas import tpu as pltpu
from jax.sharding import PartitionSpec as P

HEADS = 16
HEAD_DIM = 72
RANK = 16
ADAPTERS = 8
LORA = RANK * ADAPTERS
LANES = 128
EPS = 1e-06
SCALE = HEAD_DIM ** (-0.5)
BIG = 1e30
LOG2E = 1.4426950408889634
VMEM = 61 * 1024 * 1024

MESH = pl.DeviceIdType.MESH
bf16 = jnp.bfloat16
f32 = jnp.float32


def nn(a, b):
    return jnp.dot(a, b, preferred_element_type=f32)


def nt(a, b):
    return lax.dot_general(a, b, (((1,), (1,)), ((), ())), preferred_element_type=f32)


def tn(a, b):
    return lax.dot_general(a, b, (((0,), (0,)), ((), ())), preferred_element_type=f32)


def up128(n):
    return -(-n // LANES) * LANES


def lane_ids(rows):
    return lax.broadcasted_iota(jnp.int32, (rows, LANES), 1)


def norm_parts(x):
    center = jnp.mean(x, axis=-1, keepdims=True)
    xc = x - center
    r = lax.rsqrt(jnp.mean(xc * xc, axis=-1, keepdims=True) + EPS)
    return xc * r, r


def norm_back(dn, gain, nh, r):
    gh = dn * gain
    a = jnp.mean(gh, axis=-1, keepdims=True)
    b = jnp.mean(gh * nh, axis=-1, keepdims=True)
    return r * (gh - a - nh * b)


def column_mask(aid):
    return (lane_ids(aid.shape[0]) // RANK == aid).astype(f32)


class Spot:
    def __init__(self, nz):
        dp = lax.axis_index("dp")
        self.nz = nz
        self.x = lax.axis_index("seq")
        self.z, self.y, self.c = dp // 4, (dp // 2) % 2, dp % 2
        self.xn = self.device(1 - self.x, self.y, self.z, self.c)
        self.yn = self.device(self.x, 1 - self.y, self.z, self.c)
        self.sib = self.device(self.x, self.y, self.z, 1 - self.c)
        self.zs = [None] + [self.device(self.x, self.y, self.zk(k), self.c) for k in range(1, nz)]
        flip = self.z // 2
        self.inner = self.z + flip * (3 - 2 * self.z)
        self.zr = [m + flip * (3 - 2 * m) for m in (self.inner, 1 - self.inner, 2, 3)]
        self.zp = [self.device(self.x, self.y, z, self.c) for z in self.zr]

    def device(self, x, y, z, c):
        return ((z * 2 + y) * 2 + c, x)

    def shard(self, x, y, z):
        return (x * self.nz + z) * 4 + y * 2 + self.c

    def zk(self, k):
        return (self.z + k) % self.nz

    def barrier(self):
        peers = [self.xn, self.yn, self.sib] + self.zs[1:]
        sem = pltpu.get_barrier_semaphore()
        for peer in peers:
            pl.semaphore_signal(sem, inc=1, device_id=peer, device_id_type=MESH)
        pl.semaphore_wait(sem, len(peers))


def remote(src, dst, send, recv, device):
    return pltpu.make_async_remote_copy(
        src_ref=src, dst_ref=dst, send_sem=send, recv_sem=recv, device_id=device, device_id_type=MESH
    )


class Gather:
    kinds = [(kind, r) for r in range(4) for kind in "zxyd"]

    def __init__(self, spot, parts, ins, outs, send, recv, core, own):
        self.s, self.parts, self.ins, self.outs = spot, parts, ins, outs
        self.send, self.recv, self.core, self.own = send, recv, core, own
        self.slot = {}
        for kind, r in self.kinds:
            for to in self.targets(kind, r):
                self.slot[kind, r, to] = len(self.slot)

    @staticmethod
    def scratch(nz, count):
        dma = pltpu.SemaphoreType.DMA
        return [dma((count, 36)), dma((count, 4 * nz)), dma((count,)), dma((count,))]

    def targets(self, kind, r):
        if kind == "z":
            return (["z1", "z2", "z3"] if r == 0 else []) + ["x", "y", "s"]
        if kind == "x":
            return (["y"] if r in (0, 3) else []) + ["s"]
        if kind == "d":
            return {0: ["z1", "iz2"], 2: ["iz1"]}.get(r, []) + ["s"]
        return ["s"]

    def index(self, kind, r):
        s = self.s
        x = 1 - s.x if kind in "xd" else s.x
        y = 1 - s.y if kind in "yd" else s.y
        return s.shard(x, y, s.zr[r])

    def place(self, g, index):
        a, start, size = self.parts[g]
        if size == self.outs[a].shape[2]:
            return self.outs[a].at[index]
        return self.outs[a].at[index, :, pl.ds(start, size)]

    def source(self, g, kind, r):
        if (kind, r) != ("z", 0):
            return self.place(g, self.index(kind, r))
        a, start, size = self.parts[g]
        if size == self.ins[a].shape[1]:
            return self.ins[a]
        return self.ins[a].at[:, pl.ds(start, size)]

    def arrival(self, g, kind, r):
        return self.recv.at[g, "zxyd".index(kind) * 4 + r]

    def copy(self, g, kind, r, to):
        s = self.s
        if to == "s":
            recv, device = self.core.at[g], s.sib
        elif to == "x":
            recv, device = self.arrival(g, "x", r), s.xn
        elif to == "y":
            recv, device = self.arrival(g, "y" if kind == "z" else "d", r), s.yn
        else:
            i = int(to[-1])
            if kind == "z":
                there = i if i < 2 else 3 - s.inner
            else:
                there = 1 if to == "z1" else 2
            recv, device = self.arrival(g, kind, there), s.zp[i]
        send = self.send.at[g, self.slot[kind, r, to]]
        return remote(self.source(g, kind, r), self.place(g, self.index(kind, r)), send, recv, device)

    def each(self, g, kind, r, act):
        for to in self.targets(kind, r):
            if to[0] == "i":
                @pl.when(self.s.inner == 1)
                def _(to=to):
                    act(self.copy(g, kind, r, to))
            else:
                act(self.copy(g, kind, r, to))

    def local(self, g):
        return pltpu.make_async_copy(self.source(g, "z", 0), self.place(g, self.index("z", 0)), self.own.at[g])

    def arrive(self, g, kind, r):
        if (kind, r) == ("z", 0):
            self.local(g).start()
        else:
            ref = self.place(g, self.index(kind, r))
            remote(ref, ref, self.send.at[g, 0], self.arrival(g, kind, r), self.s.xn).wait_recv()
        self.each(g, kind, r, lambda copy: copy.start())

    def end(self, g):
        a, start, size = self.parts[g]
        n = self.outs[a].shape[0] // 2
        ref = self.outs[a].at[pl.ds(0, n), :, pl.ds(start, size)]
        if size == self.outs[a].shape[2]:
            ref = self.outs[a].at[pl.ds(0, n)]
        remote(ref, ref, self.send.at[g, 0], self.core.at[g], self.s.sib).wait_recv()
        self.local(g).wait()
        for kind, r in self.kinds:
            self.each(g, kind, r, lambda copy: copy.wait_send())

    def actions(self):
        n = len(self.parts)
        out = []
        for t in range(n + 4):
            if t < n:
                out.append((self.arrive, t, "z", 0))
            if 0 <= t - 1 < n:
                out += [(self.arrive, t - 1, "z", r) for r in (1, 2, 3)]
            if 0 <= t - 2 < n:
                out += [(self.arrive, t - 2, kind, r) for r in (0, 3, 1, 2) for kind in "xy"]
            if 0 <= t - 3 < n:
                out += [(self.arrive, t - 3, "d", r) for r in (0, 3, 2, 1)]
            if 0 <= t - 4 < n:
                out.append((self.end, t - 4))
        return out


class Swap:
    def __init__(self, spot, mine, got, sems, slot=None):
        self.s, self.mine, self.got, self.sems = spot, mine, got, sems
        self.slot = spot.x if slot is None else slot

    def copies(self):
        s = self.s
        here = pltpu.make_async_copy(self.mine.at[s.x], self.got.at[s.x], self.sems.at[0])
        there = remote(self.mine.at[1 - s.x], self.got.at[self.slot], self.sems.at[1], self.sems.at[2], s.xn)
        return here, there

    def start(self):
        for copy in self.copies():
            copy.start()

    def end(self):
        here, there = self.copies()
        here.wait()
        ref = self.got.at[1 - self.s.x]
        remote(ref, ref, self.sems.at[1], self.sems.at[2], self.s.xn).wait_recv()
        there.wait_send()


def run_actions(actions, step, steps):
    for t in range(steps):
        a, b = len(actions) * t // steps, len(actions) * (t + 1) // steps
        if a == b:
            continue

        @pl.when(step == t)
        def _(a=a, b=b):
            for action in actions[a:b]:
                action[0](*action[1:])


class Reduce:
    def __init__(self, spot, data, result, refs):
        self.s, self.data, self.result = spot, data, result
        self.r1, self.s1, self.r2, self.s2, self.r3, self.s3, self.r4, self.total = refs[:8]
        self.send, self.recv, self.out = refs[8:]

    @staticmethod
    def scratch(nz, width):
        def v(*dims):
            return pltpu.VMEM((*dims, 8, width), bf16)
        dma = pltpu.SemaphoreType.DMA
        n = 5 + 2 * (nz - 1)
        return [v(2, 2 * nz), v(2, 2 * nz), v(2, nz), v(2, nz), v(nz, 2), v(2), v(1), v(2, 2 * nz),
                dma((n,)), dma((n,)), dma((1,))]

    def pair(self, i, src, dst, device):
        return remote(src, dst, self.send.at[i], self.recv.at[i], device)

    def to_core(self):
        return self.pair(0, self.data.at[1 - self.s.c], self.r1, self.s.sib)

    def to_y(self):
        nz = self.s.nz
        return self.pair(1, self.s1.at[:, pl.ds((1 - self.s.y) * nz, nz)], self.r2, self.s.yn)

    def to_x(self):
        return self.pair(2, self.s3.at[1 - self.s.x], self.r4.at[0], self.s.xn)

    def to_z(self, k):
        s = self.s
        return self.pair(4 + k, self.s2.at[:, s.zk(k)], self.r3.at[s.z], s.zs[k])

    def from_z(self, k):
        s = self.s
        ref = self.r3.at[s.zk(k)]
        return remote(ref, ref, self.send.at[4 + s.nz - k], self.recv.at[4 + s.nz - k], s.zs[k])

    def back_z(self, k):
        s = self.s
        ref = self.total.at[s.c, s.y * s.nz + s.z]
        return self.pair(4 + s.nz - 1 + k, ref, ref, s.zs[k])

    def from_back_z(self, k):
        s = self.s
        i = 4 + s.nz - 1 + s.nz - k
        ref = self.total.at[s.c, s.y * s.nz + s.zk(k)]
        return remote(ref, ref, self.send.at[i], self.recv.at[i], s.zs[k])

    def back_y(self, y):
        s = self.s
        ref = self.total.at[s.c, pl.ds(y * s.nz, s.nz)]
        return self.pair(3, ref, ref, s.yn)

    def back_core(self, c):
        ref = self.total.at[c]
        return self.pair(4, ref, ref, self.s.sib)

    def one(self):
        self.to_core().start()

    def two(self):
        s, nz = self.s, self.s.nz
        self.to_core().wait_recv()

        def add(i, c):
            x, b = i // (2 * nz), i % (2 * nz)
            self.s1[x, b] = (self.data[s.c, x, b].astype(f32) + self.r1[x, b].astype(f32)).astype(bf16)
            return c
        lax.fori_loop(0, 4 * nz, add, 0)
        self.to_y().start()

    def three(self):
        s, nz = self.s, self.s.nz
        self.to_y().wait_recv()

        def add(i, c):
            x, b = i // nz, i % nz
            self.s2[x, b] = (self.s1[x, s.y * nz + b].astype(f32) + self.r2[x, b].astype(f32)).astype(bf16)
            return c
        lax.fori_loop(0, 2 * nz, add, 0)
        for k in range(1, nz):
            self.to_z(k).start()

    def four(self):
        s, nz = self.s, self.s.nz
        for k in range(1, nz):
            self.from_z(k).wait_recv()
        for x in range(2):
            v = self.s2[x, s.z].astype(f32)
            for k in range(1, nz):
                v = v + self.r3[s.zk(k), x].astype(f32)
            self.s3[x] = v.astype(bf16)
        self.to_x().start()

    def five(self):
        s, nz = self.s, self.s.nz
        self.to_x().wait_recv()
        v = self.s3[s.x].astype(f32) + self.r4[0].astype(f32)
        self.total[s.c, s.y * s.nz + s.z] = v.astype(bf16)
        for k in range(1, nz):
            self.back_z(k).start()

    def six(self):
        for k in range(1, self.s.nz):
            self.from_back_z(k).wait_recv()
        self.back_y(self.s.y).start()

    def seven(self):
        self.back_y(1 - self.s.y).wait_recv()
        self.back_core(self.s.c).start()

    def end(self):
        s = self.s
        self.back_core(1 - s.c).wait_recv()
        out = pltpu.make_async_copy(self.total, self.result, self.out.at[0])
        out.start()
        out.wait()
        self.to_core().wait_send()
        self.to_x().wait_send()
        self.to_y().wait_send()
        for k in range(1, s.nz):
            self.to_z(k).wait_send()
            self.back_z(k).wait_send()
        self.back_y(s.y).wait_send()
        self.back_core(s.c).wait_send()

    def actions(self):
        return [(f,) for f in (self.one, self.two, self.three, self.four, self.five, self.six, self.seven, self.end)]


def front_kernel(nz, na, *refs):
    shards, (tokens, vec, aid_ref, pic_ref), refs = refs[:na], refs[na:na + 4], refs[na + 4:]
    wholes, (x_out, vec_out, qkv_out, n1_out, h_out), refs = refs[:na], refs[na:na + 5], refs[na + 5:]
    (xbuf, vbuf, nbuf, wbuf, abuf, bbuf, n1, hbuf, heads, sems, wsem, osem, *refs) = refs
    n, d = nz * 4, xbuf.shape[2]
    count, tm = 2 * xbuf.shape[1], 512
    ds = wbuf.shape[3]
    nh = ds // HEAD_DIM
    spot = Spot(nz)
    spot.barrier()
    gather = Gather(spot, [(k, 0, a.shape[1]) for k, a in enumerate(shards)], shards, wholes, *refs)
    run = Steps(gather.actions())
    vec_here = pltpu.make_async_copy(vec, vbuf.at[spot.x], sems.at[0])
    vec_there = remote(vec, vbuf.at[spot.x], sems.at[1], sems.at[2], spot.xn)
    row_here = pltpu.make_async_copy(tokens.at[spot.x], xbuf.at[spot.x], sems.at[3])
    row_there = remote(tokens.at[1 - spot.x], xbuf.at[spot.x], sems.at[4], sems.at[5], spot.xn)
    vec_here.start()
    vec_there.start()
    run.step(2)
    row_here.start()
    row_there.start()
    run.step(13)

    vec_here.wait()
    got = vbuf.at[1 - spot.x]
    remote(got, got, sems.at[1], sems.at[2], spot.xn).wait_recv()
    row_here.wait()
    got = xbuf.at[1 - spot.x]
    remote(got, got, sems.at[4], sems.at[5], spot.xn).wait_recv()
    gain, shift = (jnp.concatenate([vbuf[j, k:k + 1, :ds] for j in range(2)], axis=1).astype(f32) for k in (4, 5))
    keep = [pltpu.make_async_copy(xbuf, x_out, osem.at[0]), pltpu.make_async_copy(vbuf, vec_out, osem.at[1])]
    for copy in keep:
        copy.start()
    for half in range(2):
        def norm_step(i, carry, half=half):
            nhat, _ = norm_parts(xbuf[half, pl.ds(i * 256, 256), :].astype(f32))
            n1[pl.ds(half * (count // 2) + i * 256, 256), :d] = (nhat * gain + shift).astype(bf16)
            return carry
        lax.fori_loop(0, count // 512, norm_step, 0)
        run.step(4)
    keep.append(pltpu.make_async_copy(n1.at[:, pl.ds(0, d)], n1_out, osem.at[2]))
    keep[-1].start()

    run.until(0)
    small = pltpu.make_async_copy(wholes[0], nbuf, sems.at[6])
    small.start()
    small.wait()
    each = LORA // 2
    for m in range(3):
        for j in range(2):
            rows = slice(j * each, (j + 1) * each)
            one = nbuf[j * n:(j + 1) * n].reshape(10 * each, d)
            abuf[m, rows, :] = one[m * each:(m + 1) * each]
            for i in range(2):
                bbuf[m, i, rows, :] = one[(5 + m) * each:(6 + m) * each, i * ds:(i + 1) * ds]

    def fetch(p, j):
        return pltpu.make_async_copy(wholes[1 + p].at[pl.ds(j * n, n)], wbuf.at[j], wsem.at[j])

    blocks = []
    for p in range(3):
        run.until(1 + p)
        for j in range(2):
            fetch(p, j).start()
        for i in range(count // tm):
            rows = pl.ds(i * tm, tm)
            h = (nt(n1[rows, :d], abuf[p]) * column_mask(aid_ref[rows, :])).astype(bf16)
            hbuf[p, rows, :] = h
            n1[rows, d:] = (0.5 * h.astype(f32)).astype(bf16)
        for j in range(2):
            fetch(p, j).wait()
            bias = vbuf[j, p // 2:p // 2 + 1, :ds].astype(f32) if p != 1 else 0.0

            def step(i, carry, p=p, j=j, bias=bias):
                rows = pl.ds(i * tm, tm)
                run.within(i, 1, count // tm, 3)
                w = jnp.concatenate([wbuf[j].reshape(d, ds), bbuf[p, j]])
                y = (nn(n1[rows, :], w) + bias).astype(bf16)
                place = lax.broadcasted_iota(jnp.int32, (tm, LANES), 1) - HEAD_DIM
                same = place == pic_ref[rows, :]
                if p == 0:
                    extra = jnp.where(same, 1.0, 0.0)
                elif p == 1:
                    extra = jnp.where((place >= 0) & (place < 16) & jnp.logical_not(same), -BIG, 0.0)
                else:
                    extra = jnp.where((place == 0) | (place == 1), 1.0, 0.0)
                extra = extra.astype(bf16)[:, HEAD_DIM:]
                for h in range(nh):
                    heads[p, j * nh + h, rows, :HEAD_DIM] = y[:, h * HEAD_DIM:(h + 1) * HEAD_DIM]
                    heads[p, j * nh + h, rows, HEAD_DIM:] = extra
                return carry
            lax.fori_loop(0, count // tm, step, 0)
            which = pl.ds(j * nh, nh)
            blocks.append(pltpu.make_async_copy(heads.at[p, which], qkv_out.at[p, which], osem.at[4 + 2 * p + j]))
            blocks[-1].start()
            run.step(3)
    keep.append(pltpu.make_async_copy(hbuf, h_out, osem.at[3]))
    keep[-1].start()
    run.rest()
    for copy in keep + blocks:
        copy.wait()
    vec_there.wait_send()
    row_there.wait_send()


def front_call(nz, shards, tokens, vec, aid, pic):
    na = len(shards)
    dma = pltpu.SemaphoreType.DMA
    count, d = 2 * tokens.shape[1], tokens.shape[2]
    ds = shards[1].shape[1]
    full = pl.BlockSpec(memory_space=pltpu.VMEM)

    def v(*shape):
        return pltpu.VMEM(shape, bf16)

    def out(*shape):
        return jax.ShapeDtypeStruct(shape, bf16)

    return pl.pallas_call(
        partial(front_kernel, nz, na),
        in_specs=any_specs(na + 2) + [full, full],
        out_specs=any_specs(na + 5),
        out_shape=gathered(nz, shards) + [
            out(*tokens.shape), out(2, *vec.shape), out(3, HEADS, count, LANES), out(count, d), out(3, count, LORA)],
        scratch_shapes=[
            v(*tokens.shape), v(2, *vec.shape), v(8 * nz, *shards[0].shape), v(2, 4 * nz, *shards[1].shape),
            v(3, LORA, d), v(3, 2, LORA, ds), v(count, d + LORA), v(3, count, LORA), v(3, HEADS, count, LANES),
            dma((7,)), dma((2,)), dma((10,))] + Gather.scratch(nz, na),
        compiler_params=pltpu.CompilerParams(collective_id=1, has_side_effects=True, vmem_limit_bytes=VMEM),
        name="front",
    )(*shards, tokens, vec, aid, pic)


def any_specs(n):
    return [pl.BlockSpec(memory_space=pl.ANY)] * n


def gathered(nz, arrays):
    return [jax.ShapeDtypeStruct((8 * nz,) + a.shape, a.dtype) for a in arrays]


def finish_kernel(nz, g_ref, d_ref, total_ref, got_ref, *refs):
    spot = Spot(nz)
    spot.barrier()
    reduce = Reduce(spot, g_ref, total_ref, refs[:-1])
    sems = refs[-1]
    there = remote(d_ref.at[1 - spot.x], got_ref, sems.at[0], sems.at[1], spot.xn)
    reduce.one()
    there.start()
    for f in reduce.actions()[1:]:
        f[0]()
    there.wait()


def finish_call(nz, g, d):
    width = g.shape[-1]
    dma = pltpu.SemaphoreType.DMA
    return pl.pallas_call(
        partial(finish_kernel, nz),
        in_specs=[pl.BlockSpec(memory_space=pltpu.VMEM), pl.BlockSpec(memory_space=pl.ANY)],
        out_specs=any_specs(2),
        out_shape=[
            jax.ShapeDtypeStruct((2,) + g.shape[2:], bf16), jax.ShapeDtypeStruct(d.shape[1:], bf16)],
        scratch_shapes=Reduce.scratch(nz, width) + [dma((2,))],
        compiler_params=pltpu.CompilerParams(collective_id=5, has_side_effects=True, vmem_limit_bytes=40 * 2**20),
        name="finish",
    )(g, d)


class Steps:
    def __init__(self, actions):
        self.actions = list(actions)

    def step(self, count):
        for action in self.actions[:count]:
            action[0](*action[1:])
        del self.actions[:count]

    def rest(self):
        self.step(len(self.actions))

    def until(self, part):
        ends = [k for k, action in enumerate(self.actions) if action[0].__name__ == "end" and action[1] == part]
        if ends:
            self.step(ends[0] + 1)

    def within(self, i, first, last, count):
        for t in range(first, last):
            pl.when(i == t)(partial(self.step, count))


class Quiet:
    args = ()
    outs = ()
    steps = 1

    def split(self, refs, own):
        a, b = len(self.args), len(self.outs)
        return refs[:a], refs[a:a + own], refs[a + own:a + own + b], refs[a + own + b:]

    def in_specs(self):
        return any_specs(len(self.args))

    def out_specs(self):
        return any_specs(len(self.outs))

    def out_shape(self):
        return list(self.outs)

    def scratch(self):
        return []

    def params(self):
        return pltpu.CompilerParams(vmem_limit_bytes=VMEM)

    def run(self, step, ins, outs, refs):
        pass

    def close(self, step, ins, outs, refs):
        pass

    def begin(self, ins, outs, refs):
        return Steps([])


class Fetch(Quiet):
    def __init__(self, nz, shards, parts, cid, halves=None):
        self.nz, self.parts, self.cid, self.na = nz, parts, cid, len(shards)
        self.args = tuple(shards) + (() if halves is None else (halves,))
        self.outs = gathered(nz, shards) + ([] if halves is None else [jax.ShapeDtypeStruct(halves.shape, halves.dtype)])

    def scratch(self):
        return Gather.scratch(self.nz, len(self.parts)) + [pltpu.SemaphoreType.DMA((3,))]

    def params(self):
        return pltpu.CompilerParams(vmem_limit_bytes=VMEM, collective_id=self.cid, has_side_effects=True)

    def make(self, ins, outs, refs):
        spot = Spot(self.nz)
        gather = Gather(spot, self.parts, ins[:self.na], outs[:self.na], *refs[-5:-1])
        swap = Swap(spot, ins[-1], outs[-1], refs[-1]) if len(ins) > self.na else None
        return spot, gather, swap

    def begin(self, ins, outs, refs):
        spot, gather, _ = self.make(ins, outs, refs)
        spot.barrier()
        return Steps(gather.actions())

    def run(self, step, ins, outs, refs):
        spot, gather, swap = self.make(ins, outs, refs)

        @pl.when(step == 0)
        def _():
            spot.barrier()
            if swap:
                swap.start()
        run_actions(gather.actions()[:-4], step, self.steps)

    def close(self, step, ins, outs, refs):
        _, gather, swap = self.make(ins, outs, refs)

        @pl.when(step == self.steps - 1)
        def _():
            for action in gather.actions()[-4:]:
                action[0](*action[1:])
            if swap:
                swap.end()


class Settle(Quiet):
    def __init__(self, nz, g, halves, cid):
        self.nz, self.width, self.cid = nz, g.shape[-1], cid
        self.args = (g, halves)
        self.outs = [jax.ShapeDtypeStruct((2,) + g.shape[2:], bf16), jax.ShapeDtypeStruct(halves.shape, halves.dtype)]

    def in_specs(self):
        return [pl.BlockSpec(memory_space=pltpu.VMEM), pl.BlockSpec(memory_space=pl.ANY)]

    def scratch(self):
        return Reduce.scratch(self.nz, self.width) + [pltpu.SemaphoreType.DMA((3,))]

    def params(self):
        return pltpu.CompilerParams(vmem_limit_bytes=VMEM, collective_id=self.cid, has_side_effects=True)

    def make(self, ins, outs, refs):
        spot = Spot(self.nz)
        refs = refs[-12:]
        return spot, Reduce(spot, ins[0], outs[0], refs[:-1]), Swap(spot, ins[1], outs[1], refs[-1])

    def run(self, step, ins, outs, refs):
        spot, reduce, swap = self.make(ins, outs, refs)
        when = [0, 1, 4, 7, 9, 11, 13]

        @pl.when(step == 0)
        def _():
            spot.barrier()
        for (f,), t in zip(reduce.actions(), when):
            pl.when(step == t)(f)

        @pl.when(step == 4)
        def _():
            swap.start()

    def close(self, step, ins, outs, refs):
        _, reduce, swap = self.make(ins, outs, refs)

        @pl.when(step == self.steps - 1)
        def _():
            reduce.end()
            swap.end()


def qkv_kernel(nh, tm, x_ref, w_ref, at_ref, b_ref, bias_ref, vec_ref, aid_ref, pic_ref, out_ref, n1_ref, h_ref):
    p = pl.program_id(0)
    j = pl.program_id(1)
    tokens = x_ref.shape[0]

    @pl.when((p == 0) & (j == 0))
    def _():
        def norm_step(i, c):
            rows = pl.ds(i * tm, tm)
            nhat, _ = norm_parts(x_ref[rows, :].astype(f32))
            n1_ref[rows, :] = (nhat * vec_ref[4:5, :] + vec_ref[5:6, :]).astype(bf16)
            return c
        lax.fori_loop(0, tokens // tm, norm_step, 0)

    @pl.when(j == 0)
    def _():
        def hidden_step(i, c):
            rows = pl.ds(i * tm, tm)
            h = nt(n1_ref[rows, :], at_ref[0]) * column_mask(aid_ref[rows, :])
            h_ref[0, rows, :] = h.astype(bf16)
            return c
        lax.fori_loop(0, tokens // tm, hidden_step, 0)

    def step(i, c):
        rows = pl.ds(i * tm, tm)
        y = nn(n1_ref[rows, :], w_ref[0, 0])
        y = y + 0.5 * nn(h_ref[0, rows, :], b_ref[0, 0]) + bias_ref[0, 0]
        slot = lane_ids(tm) - HEAD_DIM
        pic = pic_ref[rows, :]
        same = slot == pic
        in_slots = (slot >= 0) & (slot < 16)
        q_aug = jnp.where(same, 1.0, 0.0)
        k_aug = jnp.where(in_slots & jnp.logical_not(same), -BIG, 0.0)
        v_aug = jnp.where((slot == 0) | (slot == 1), 1.0, 0.0)
        aug = jnp.where(p == 0, q_aug, jnp.where(p == 1, k_aug, v_aug))[:, HEAD_DIM:]
        for h in range(nh):
            head = y[:, h * HEAD_DIM:(h + 1) * HEAD_DIM]
            out_ref[0, h, rows, :HEAD_DIM] = head.astype(bf16)
            out_ref[0, h, rows, HEAD_DIM:] = aug.astype(bf16)
        return c
    lax.fori_loop(0, tokens // tm, step, 0)


def qkv_call(x, w, at, bq, bias, vec, aid, pic):
    tokens, d = x.shape
    s = w.shape[1]
    nh = HEADS // s
    tm = min(256, tokens)
    return pl.pallas_call(
        partial(qkv_kernel, nh, tm),
        grid=(3, s),
        in_specs=[
            pl.BlockSpec((tokens, d), lambda p, j: (0, 0)),
            pl.BlockSpec((1, 1, d, d // s), lambda p, j: (p, j, 0, 0)),
            pl.BlockSpec((1, LORA, d), lambda p, j: (p, 0, 0)),
            pl.BlockSpec((1, 1, LORA, nh * HEAD_DIM), lambda p, j: (p, j, 0, 0)),
            pl.BlockSpec((1, 1, 1, nh * HEAD_DIM), lambda p, j: (p, j, 0, 0)),
            pl.BlockSpec(vec.shape, lambda p, j: (0, 0)),
            pl.BlockSpec((tokens, 1), lambda p, j: (0, 0)),
            pl.BlockSpec((tokens, 1), lambda p, j: (0, 0)),
        ],
        out_specs=[
            pl.BlockSpec((1, nh, tokens, LANES), lambda p, j: (p, j, 0, 0)),
            pl.BlockSpec((tokens, d), lambda p, j: (0, 0)),
            pl.BlockSpec((1, tokens, LORA), lambda p, j: (p, 0, 0)),
        ],
        out_shape=[
            jax.ShapeDtypeStruct((3, HEADS, tokens, LANES), bf16),
            jax.ShapeDtypeStruct((tokens, d), bf16),
            jax.ShapeDtypeStruct((3, tokens, LORA), bf16),
        ],
        compiler_params=pltpu.CompilerParams(vmem_limit_bytes=VMEM),
        name="qkv",
    )(x, w, at, bq, bias, vec, aid, pic)


def attn_fwd_kernel(tq, comm, q_ref, k_ref, v_ref, *refs):
    ins, (p_ref, o_ref), outs, refs = comm.split(refs, 2)
    comm.run(pl.program_id(0), ins, outs, refs)

    for i in range(q_ref.shape[2] // tq):
        rows = pl.ds(i * tq, tq)
        s = nt(q_ref[0, 0, rows, :], k_ref[0, 0])
        top = jnp.max(s, axis=-1, keepdims=True)
        p = jnp.exp2((s - top) * (SCALE * LOG2E)).astype(bf16)
        o = nn(p, v_ref[0, 0])
        inv = 1.0 / o[:, HEAD_DIM:HEAD_DIM + 1]
        p_ref[0, rows, :] = (p.astype(f32) * inv).astype(bf16)
        o_ref[0, rows, :] = (o * inv).astype(bf16)
    comm.close(pl.program_id(0), ins, outs, refs)


def attn_fwd_call(qkv, kv, off, comm):
    tokens, keys = qkv.shape[2], kv.shape[2]
    tq = min(512, tokens)
    comm.steps = HEADS
    return pl.pallas_call(
        partial(attn_fwd_kernel, tq, comm),
        grid=(HEADS,),
        in_specs=[
            pl.BlockSpec((1, 1, tokens, LANES), lambda h: (0, h, 0, 0)),
            pl.BlockSpec((1, 1, keys, LANES), lambda h: (off, h, 0, 0)),
            pl.BlockSpec((1, 1, keys, LANES), lambda h: (off + 1, h, 0, 0)),
        ] + comm.in_specs(),
        out_specs=[
            pl.BlockSpec((1, tokens, keys), lambda h: (h, 0, 0)),
            pl.BlockSpec((1, tokens, LANES), lambda h: (h, 0, 0)),
        ] + comm.out_specs(),
        out_shape=[
            jax.ShapeDtypeStruct((HEADS, tokens, keys), bf16),
            jax.ShapeDtypeStruct((HEADS, tokens, LANES), bf16),
        ] + comm.out_shape(),
        scratch_shapes=comm.scratch(),
        compiler_params=comm.params(),
        name="attn_fwd",
    )(qkv, kv, kv, *comm.args)


def attn_bwd_kernel(tq, comm, q_ref, k_ref, v_ref, p_ref, o_ref, do_ref, *refs):
    ins, (dq_ref, dk_ref, dv_ref), outs, (ds_ref, da_ref, *refs) = comm.split(refs, 3)
    comm.run(pl.program_id(0), ins, outs, refs)

    for i in range(q_ref.shape[2] // tq):
        rows = pl.ds(i * tq, tq)
        lane = lane_ids(tq)
        do = jnp.where(lane < HEAD_DIM, do_ref[0, rows, :].astype(f32), 0.0)
        delta = jnp.sum(do * o_ref[0, rows, :].astype(f32), axis=-1, keepdims=True)
        hi = delta.astype(bf16).astype(f32)
        do = jnp.where(lane == HEAD_DIM, -hi, jnp.where(lane == HEAD_DIM + 1, hi - delta, do)).astype(bf16)
        da_ref[rows, :] = do
        dp = nt(do, v_ref[0, 0])
        ds = (p_ref[0, rows, :].astype(f32) * dp).astype(bf16)
        ds_ref[rows, :] = ds
        dq_ref[0, rows, :] = (nn(ds, k_ref[0, 0]) * SCALE).astype(bf16)
    dv_ref[0] = nn(da_ref[...].T, p_ref[0]).T.astype(bf16)
    dk_ref[0] = (nn(q_ref[0, 0].T, ds_ref[...]).T * SCALE).astype(bf16)
    comm.close(pl.program_id(0), ins, outs, refs)


def attn_bwd_call(qkv, kv, off, probs, out, d_out, comm):
    tokens, keys = qkv.shape[2], kv.shape[2]
    tq = min(256, tokens)
    comm.steps = HEADS
    return pl.pallas_call(
        partial(attn_bwd_kernel, tq, comm),
        grid=(HEADS,),
        in_specs=[
            pl.BlockSpec((1, 1, tokens, LANES), lambda h: (0, h, 0, 0)),
            pl.BlockSpec((1, 1, keys, LANES), lambda h: (off, h, 0, 0)),
            pl.BlockSpec((1, 1, keys, LANES), lambda h: (off + 1, h, 0, 0)),
            pl.BlockSpec((1, tokens, keys), lambda h: (h, 0, 0)),
            pl.BlockSpec((1, tokens, LANES), lambda h: (h, 0, 0)),
            pl.BlockSpec((1, tokens, LANES), lambda h: (h, 0, 0)),
        ] + comm.in_specs(),
        out_specs=[
            pl.BlockSpec((1, tokens, LANES), lambda h: (h, 0, 0)),
            pl.BlockSpec((1, keys, LANES), lambda h: (h, 0, 0)),
            pl.BlockSpec((1, keys, LANES), lambda h: (h, 0, 0)),
        ] + comm.out_specs(),
        out_shape=[
            jax.ShapeDtypeStruct((HEADS, tokens, LANES), bf16),
            jax.ShapeDtypeStruct((HEADS, keys, LANES), bf16),
            jax.ShapeDtypeStruct((HEADS, keys, LANES), bf16),
        ] + comm.out_shape(),
        scratch_shapes=[pltpu.VMEM((tokens, keys), bf16), pltpu.VMEM((tokens, LANES), bf16)] + comm.scratch(),
        compiler_params=comm.params(),
        name="attn_bwd",
    )(qkv, kv, kv, probs, out, d_out, *comm.args)


def gelu_parts(z):
    c = 0.7978845608028654
    z2 = z * z
    t = jnp.tanh(z * (c + (c * 0.044715) * z2))
    half = 0.5 * (1.0 + t)
    g = z * half
    dg = half + 0.5 * z * (1.0 - t * t) * (c + (3 * c * 0.044715) * z2)
    return g, dg


def mid_kernel(s, n, cuts, comm, *refs):
    own, refs = refs[:9 + 2 * comm.ready], refs[9 + 2 * comm.ready:]
    oaug_ref, x_ref, cot_ref, aid_ref, wo_ref, ab_ref, ff_ref, bup_ref, vec_ref = own[:9]
    weights = list(own[9:])
    ins, (mixed_ref, dmid_ref, do_ref, pack_ref), outs, refs = comm.split(refs, 4)
    (obuf, xbuf, dybuf, wobuf, ocat, n2buf, mid, acc, dn2, hidden, wofull, ubuf, dbuf, ga, gb, isem, wsem, osem,
     go, cotbuf, lsem, *comm_refs) = refs
    weights += list(outs[:2 * (len(cuts) - comm.ready)])
    tokens, d = xbuf.shape
    ds = d // s
    bo, bd, gain2, shift2 = vec_ref[2:3, :], vec_ref[3:4, :], vec_ref[6:7, :], vec_ref[7:8, :]
    at_o, at_u, b_o, b_d = (ab_ref.at[k] for k in range(4))
    ta, tm = min(256, tokens), min(512, tokens)
    chunks = [(c, j) for c in range(len(cuts)) for j in range(s)]

    def load(i):
        rows = pl.ds(i * ta, ta)
        for k, (src, dst) in enumerate(((oaug_ref.at[:, rows], obuf.at[:, rows]), (x_ref.at[rows], xbuf.at[rows]),
                                        (cot_ref.at[rows], cotbuf.at[rows]))):
            yield pltpu.make_async_copy(src, dst, isem.at[i, k])

    def save(i):
        rows = pl.ds(i * ta, ta)
        for k, (src, dst) in enumerate(((xbuf.at[rows], mixed_ref.at[rows]), (mid.at[rows], dmid_ref.at[rows]),
                                        (obuf.at[:, rows], do_ref.at[:, rows]))):
            yield pltpu.make_async_copy(src, dst, osem.at[i, k])

    wo_load = pltpu.make_async_copy(wo_ref, wobuf, lsem.at[0])
    def fetch(k):
        c, j = chunks[k]
        w = cuts[c][1]
        for m, (ref, buf) in enumerate(((weights[2 * c], ubuf), (weights[2 * c + 1], dbuf))):
            dst = buf.at[k % 2] if w == buf.shape[3] else buf.at[k % 2, :, :, pl.ds(0, w)]
            yield pltpu.make_async_copy(ref.at[pl.ds(j * n, n)], dst, wsem.at[k % 2, m])

    wo_load.start()
    for i in range(tokens // ta):
        for copy in load(i):
            copy.start()
    run = comm.begin(ins, outs, comm_refs)
    for copy in fetch(0):
        copy.start()
    wo_load.wait()
    run.step(4)

    wo = jnp.concatenate([wobuf[j][:, :ds] for j in range(s)], axis=1) if s > 1 else wobuf[0]
    wofull[...] = wo

    def before(i, carry):
        rows = pl.ds(i * ta, ta)
        run.within(i, 1, tokens // ta, 4)
        for copy in load(i):
            copy.wait()
        mask = column_mask(aid_ref[rows, :])
        for h in range(HEADS):
            ocat[rows, h * HEAD_DIM:(h + 1) * HEAD_DIM] = obuf[h, rows, :HEAD_DIM]
        o = ocat[rows, :]
        h_o = (nt(o, at_o[...]) * mask).astype(bf16)
        value = xbuf[rows, :].astype(f32) + nn(o, wofull[...]) + 0.5 * nn(h_o, b_o[...]) + bo
        mid[rows, :] = value
        nh2, _ = norm_parts(value)
        n2 = (nh2 * gain2 + shift2).astype(bf16)
        n2buf[rows, :d] = n2
        dy = jnp.where(aid_ref[rows, :] >= 0, cotbuf[rows, :], jnp.zeros((ta, d), bf16))
        dybuf[rows, :d] = dy
        hidden[rows, :] = h_o
        n2buf[rows, d:] = (0.5 * (nt(n2, at_u[...]) * mask).astype(bf16).astype(f32)).astype(bf16)
        dybuf[rows, d:] = (0.5 * nt(dy, b_d[...]) * mask).astype(bf16)
        return carry
    lax.fori_loop(0, tokens // ta, before, 0)

    for k, (c, j) in enumerate(chunks):
        start, w = cuts[c]
        late = k + 1 < len(chunks) and chunks[k + 1][0] >= comm.ready and chunks[k + 1][1] == 0
        if k + 1 < len(chunks) and not late:
            for copy in fetch(k + 1):
                copy.start()
        for copy in fetch(k):
            copy.wait()
        cols = slice(start, start + w)

        def chunk(i, carry, k=k, j=j, w=w, cols=cols, slot=k % 2):
            rows = pl.ds(i * tm, tm)
            run.within(i, 1, tokens // tm, 8)
            wu = jnp.concatenate([ubuf[slot, :, :, :w].reshape(d, w), ff_ref[1, j, :, cols]])
            wd = jnp.concatenate([dbuf[slot, :, :, :w].reshape(d, w), ff_ref[0, j, :, cols]])
            z = nn(n2buf[rows, :], wu) + bup_ref[j, :, cols]
            g, dgelu = gelu_parts(z)
            g = g.astype(bf16)
            dg = nn(dybuf[rows, :], wd).astype(bf16)
            dz = (dg.astype(f32) * dgelu).astype(bf16)
            if k == 0:
                acc[rows, :] = nt(g, wd)
                dn2[rows, :] = nt(dz, wu)
            else:
                acc[rows, :] += nt(g, wd)
                dn2[rows, :] += nt(dz, wu)
            more_a, more_b = tn(dybuf[rows, d:], g), tn(n2buf[rows, d:], dz)

            @pl.when(i == 0)
            def _():
                ga[:, :w] = more_a
                gb[:, :w] = more_b

            @pl.when(i > 0)
            def _():
                ga[:, :w] += more_a
                gb[:, :w] += more_b
            return carry
        lax.fori_loop(0, tokens // tm, chunk, 0)
        at = 2 * d + j * ff_ref.shape[3] + start
        pack_ref[0, :, at:at + w] = ga[:, :w].astype(bf16)
        pack_ref[1, :, at:at + w] = gb[:, :w].astype(bf16)
        run.step(8)
        if late:
            run.until(2 * (chunks[k + 1][0] - comm.ready) + 1)
            for copy in fetch(k + 1):
                copy.start()

    run.rest()

    go[...] = jnp.zeros_like(go)

    def after(i, carry):
        rows = pl.ds(i * ta, ta)
        mask = column_mask(aid_ref[rows, :])
        h_d = (acc[rows, d:] * mask).astype(bf16)
        xbuf[rows, :] = (mid[rows, :] + bd + acc[rows, :d] + 0.5 * nn(h_d, b_d[...])).astype(bf16)
        dh_u = (0.5 * dn2[rows, d:] * mask).astype(bf16)
        nh2, r2 = norm_parts(mid[rows, :])
        dy = dybuf[rows, :d]
        dmid = dy.astype(f32) + norm_back(dn2[rows, :d] + nn(dh_u, at_u[...]), gain2, nh2, r2)
        mid[rows, :] = dmid
        db = dmid.astype(bf16)
        dh_o = (0.5 * nt(db, b_o[...]) * mask).astype(bf16)
        do = (nt(db, wofull[...]) + nn(dh_o, at_o[...])).astype(bf16)
        go[0] += tn(dh_o, ocat[rows, :])
        go[1] += 0.5 * tn(hidden[rows, :], db)
        go[2] += tn(dh_u, n2buf[rows, :d])
        go[3] += 0.5 * tn(h_d, dy)
        for h in range(HEADS):
            obuf[h, rows, :HEAD_DIM] = do[:, h * HEAD_DIM:(h + 1) * HEAD_DIM]
        for copy in save(i):
            copy.start()
        return carry
    lax.fori_loop(0, tokens // ta, after, 0)
    for c, order in enumerate(((0, 2), (1, 3))):
        for k, which in enumerate(order):
            pack_ref[c, :, k * d:(k + 1) * d] = go[which].astype(bf16)
    for i in range(tokens // ta):
        for copy in save(i):
            copy.wait()


def mid_call(oaug, x, cot, aid, wo, weights, cuts, ab, ff, bup, vec, comm):
    tokens, d = x.shape
    s, ds = wo.shape[0], wo.shape[2]
    pieces = weights[0].shape[0] // s
    widest = max(w for _, w in cuts)
    fslot = ff.shape[3]
    full = pl.BlockSpec(memory_space=pltpu.VMEM)
    dma = pltpu.SemaphoreType.DMA
    comm.ready = len(weights) // 2
    tiles = tokens // min(256, tokens)

    def v(*shape, dtype=bf16):
        return pltpu.VMEM(shape, dtype)

    return pl.pallas_call(
        partial(mid_kernel, s, pieces, cuts, comm),
        in_specs=any_specs(3) + [full] + any_specs(1) + [full] * 4 + any_specs(len(weights)) + comm.in_specs(),
        out_specs=any_specs(3) + [full] + comm.out_specs(),
        out_shape=[
            jax.ShapeDtypeStruct((tokens, d), bf16),
            jax.ShapeDtypeStruct((tokens, d), f32),
            jax.ShapeDtypeStruct((HEADS, tokens, LANES), bf16),
            jax.ShapeDtypeStruct((2, LORA, 2 * d + s * fslot), bf16),
        ] + comm.out_shape(),
        scratch_shapes=[
            v(HEADS, tokens, LANES), v(tokens, d), v(tokens, d + LORA), v(s, d, ds), v(tokens, d), v(tokens, d + LORA),
            v(tokens, d, dtype=f32), v(tokens, d + LORA, dtype=f32), v(tokens, d + LORA, dtype=f32),
            v(tokens, LORA), v(d, d), v(2, pieces, d // pieces, widest), v(2, pieces, d // pieces, widest),
            v(LORA, widest, dtype=f32), v(LORA, widest, dtype=f32),
            dma((tiles, 3)), dma((2, 2)), dma((tiles, 3)), v(4, LORA, d, dtype=f32), v(tokens, d), dma((1,)),
        ] + comm.scratch(),
        compiler_params=comm.params(),
        name="mid",
    )(oaug, x, cot, aid, wo, ab, ff, bup, vec, *weights, *comm.args)


def tail_kernel(s, dq_ref, dk_ref, dv_ref, x_ref, n1_ref, h_ref, dmid_ref, aid_ref,
                wq_ref, wk_ref, wv_ref, at_ref, b_ref, vec_ref, out_ref, low_ref, pack_ref, dy_ref, ga_ref, gb_ref):
    i = pl.program_id(0)
    tm, d = x_ref.shape
    nh = HEADS // s
    ds = d // s
    mask = column_mask(aid_ref[...])

    @pl.when(i == 0)
    def _():
        ga_ref[...] = jnp.zeros_like(ga_ref)
        gb_ref[...] = jnp.zeros_like(gb_ref)

    n1 = n1_ref[...]
    dn = jnp.zeros((tm, d), f32)
    for p, (src, w_ref) in enumerate(((dq_ref, wq_ref), (dk_ref, wk_ref), (dv_ref, wv_ref))):
        dh = jnp.zeros((tm, LORA), f32)
        for j in range(s):
            for h in range(nh):
                dy_ref[p, j, :, h * HEAD_DIM:(h + 1) * HEAD_DIM] = src[j * nh + h, :, :HEAD_DIM]
            dy = dy_ref[p, j]
            dh = dh + nt(dy, b_ref[p, j])
            dn = dn + nt(dy, w_ref[j])
            gb_ref[p, j] += 0.5 * tn(h_ref[p], dy)
        dh = (0.5 * dh * mask).astype(bf16)
        dn = dn + nn(dh, at_ref[p])
        ga_ref[p] += tn(dh, n1)
    nhat, r = norm_parts(x_ref[...].astype(f32))
    out = dmid_ref[...] + norm_back(dn, vec_ref[4:5, :], nhat, r)
    out_ref[...] = out
    low_ref[...] = out.astype(bf16)

    @pl.when(i == pl.num_programs(0) - 1)
    def _():
        for p in range(3):
            pack_ref[0, :, p * d:(p + 1) * d] = ga_ref[p].astype(bf16)
            for j in range(s):
                at = p * d + j * ds
                pack_ref[1, :, at:at + ds] = gb_ref[p, j].astype(bf16)


def tail_call(dq, dk, dv, x, n1, hid, dmid, aid, wq, wk, wv, at, bq, vec):
    tokens, d = x.shape
    s = wq.shape[0]
    tm = min(256, tokens)
    full = pl.BlockSpec(memory_space=pltpu.VMEM)
    tile = pl.BlockSpec((tm, d), lambda i: (i, 0))
    heads = pl.BlockSpec((HEADS, tm, LANES), lambda i: (0, i, 0))
    return pl.pallas_call(
        partial(tail_kernel, s),
        grid=(tokens // tm,),
        in_specs=[
            heads, heads, heads, tile, tile,
            pl.BlockSpec((3, tm, LORA), lambda i: (0, i, 0)),
            tile,
            pl.BlockSpec((tm, 1), lambda i: (i, 0)),
            full, full, full, full, full, full,
        ],
        out_specs=[tile, tile, full],
        out_shape=[
            jax.ShapeDtypeStruct((tokens, d), f32),
            jax.ShapeDtypeStruct((tokens, d), bf16),
            jax.ShapeDtypeStruct((2, LORA, 3 * d), bf16),
        ],
        scratch_shapes=[
            pltpu.VMEM((3, s, tm, d // s), bf16),
            pltpu.VMEM((3, LORA, d), f32),
            pltpu.VMEM((3, s, LORA, d // s), f32),
        ],
        compiler_params=pltpu.CompilerParams(vmem_limit_bytes=VMEM),
        name="tail",
    )(dq, dk, dv, x, n1, hid, dmid, aid, wq, wk, wv, at, bq, vec)


def rows_of_adapters(a):
    t = jnp.swapaxes(a, -1, -2)
    return t.reshape(*t.shape[:-3], t.shape[-3] * t.shape[-2], t.shape[-1])


def local(tokens, cotangent, lengths, adapter_ids, w_query, w_key, w_value, w_out, w_up, w_down,
          b_query, b_value, b_out, b_up, b_down, gain_one, shift_one, gain_two, shift_two,
          qkv_a, out_a, attn_b, up_a, up_b, down_a, down_b):
    seq = lax.axis_size("seq")
    rows, part_len, d = tokens.shape
    group = seq // rows
    count = rows * part_len
    ds, fs = w_query.shape[1], w_up.shape[1]
    me = lax.axis_index("seq")
    row, chunk = me // group, me % group

    def moves(j):
        return [(a, (a % rows + j) % rows * group + a // rows) for a in range(seq)]

    def send(piece, pairs):
        return piece if all(a == b for a, b in pairs) else lax.ppermute(piece, "seq", pairs)

    def to_row(t):
        out = jnp.zeros((rows, part_len, d), t.dtype)
        for j in range(rows):
            piece = lax.dynamic_index_in_dim(t, (me + j) % rows, 0, False)
            out = lax.dynamic_update_index_in_dim(out, send(piece, moves(j)), (row - j) % rows, 0)
        return out.reshape(count, d)

    def from_row(t, dtype):
        t = t.reshape(rows, part_len, d)
        out = jnp.zeros((rows, part_len, d), dtype)
        for j in range(rows):
            piece = lax.dynamic_index_in_dim(t, (row - j) % rows, 0, False)
            pairs = [(b, a) for a, b in moves(j)]
            if not all(a == b for a, b in pairs):
                piece = piece.astype(bf16)
            got = send(piece, pairs).astype(dtype)
            out = lax.dynamic_update_index_in_dim(out, got, (me + j) % rows, 0)
        return out

    dps = lax.axis_size("dp")
    nz = dps // 4
    fast = seq == 2 and rows == 2 and nz == 4
    slot, fslot = up128(ds), up128(fs)
    step = up128(-(-fslot // max(round(fslot / 768), 1)))
    cuts = [(a, min(step, fslot - a)) for a in range(0, fslot, step)]

    def wide_to(t, n):
        return jnp.pad(t, ((0, 0), (0, n - t.shape[1])))

    wu_part, wd_part = wide_to(w_up, fslot), wide_to(w_down.T, fslot)
    ff_parts = [t[:, a:a + n] for a, n in cuts for t in (wu_part, wd_part)]
    narrow = jnp.concatenate([
        rows_of_adapters(qkv_a), rows_of_adapters(out_a)[None], rows_of_adapters(up_a)[None],
        attn_b.reshape(4, -1, d), down_b.reshape(1, -1, d)])
    wide = jnp.stack([rows_of_adapters(down_a), up_b.reshape(-1, up_b.shape[-1])])
    vec_part = jnp.stack([b_query, b_value, b_out, b_down, gain_one, shift_one, gain_two, shift_two])
    teams = [[g * group + c for c in range(group)] for g in range(rows)]

    my_len = lax.dynamic_index_in_dim(lengths, row, 0, False)
    my_ids = lax.dynamic_index_in_dim(adapter_ids, row, 0, False)
    slots = jnp.arange(my_len.shape[0], dtype=jnp.int32)
    ends = jnp.sum(jnp.where(slots[None, :] <= slots[:, None], my_len[None, :], 0), axis=1)
    pos = chunk * count + jnp.arange(count, dtype=jnp.int32)
    pic = jnp.sum((pos[:, None] >= ends[None, :]).astype(jnp.int32), axis=1, keepdims=True)
    aid = jnp.sum(jnp.where(pic == slots[None, :], my_ids[None, :], 0), axis=1, keepdims=True)
    aid = jnp.where(pos[:, None] < ends[-1], aid, -1)

    def from_halves(t):
        return jnp.swapaxes(t, 0, 1).reshape(t.shape[1], -1, t.shape[3])

    if fast:
        me_dp = lax.axis_index("dp")

        def share(t):
            flat = t.reshape(-1, t.shape[-1])
            n = flat.shape[0] // dps
            return lax.dynamic_slice_in_dim(flat, me_dp * n, n, 0)

        def whole(t):
            return t.reshape(seq, d, t.shape[2])

        small = jnp.concatenate([wide_to(vec_part, fslot), wide_to(b_up[None], fslot), jnp.zeros((7, fslot), bf16)])
        narrow, wq, wk, wv, wo, wide, x, small, qkv, n1, hid = front_call(
            nz, [share(narrow), w_query, w_key, w_value, w_out, share(wide)], tokens, small, aid, pic)
        x = x.reshape(count, d)
        narrow = from_halves(narrow.reshape(seq, 10, LORA // seq, d))
        vec = jnp.concatenate([small[k, :8, :ds] for k in range(seq)], axis=1).astype(f32)
        bup = small[:, 8:9, :fs].astype(f32)
        wq, wk, wv, wo = whole(wq), whole(wk), whole(wv), whole(wo)
        wide = from_halves(wide.reshape(seq, 2, LORA // seq, -1))

        def fetch(shards, cid, halves=None):
            return Fetch(nz, shards, [(k, 0, t.shape[1]) for k, t in enumerate(shards)], cid, halves)

        second = fetch(ff_parts[:2], 3, cotangent)
        last = fetch(ff_parts[2:], 6)
    else:
        def gather_all(shard):
            full = lax.all_gather(shard, ("seq", "dp"), axis=0, tiled=True)
            return full.reshape(seq, d, shard.shape[1])

        wq, wk, wv, wo, *weights = (gather_all(t) for t in [w_query, w_key, w_value, w_out] + ff_parts)
        narrow = lax.all_gather(narrow, "seq", axis=1, tiled=True)
        wide = lax.all_gather(wide, "seq", axis=1, tiled=True)
        vec = lax.all_gather(vec_part, "seq", axis=1, tiled=True).astype(f32)
        bup = lax.all_gather(b_up[None], "seq", axis=0, tiled=True).astype(f32)[:, None]
        x = to_row(tokens)
        cot = to_row(cotangent)
        second = last = Quiet()

    at, b = narrow[:5], narrow[5:]
    bq = jnp.swapaxes(b[:3].reshape(3, LORA, seq, ds), 1, 2)
    bias = jnp.stack([vec[0], jnp.zeros_like(vec[0]), vec[1]]).reshape(3, seq, 1, ds)
    if not fast:
        wqkv = jnp.stack([wq, wk, wv])
        qkv, n1, hid = qkv_call(x, wqkv, at, bq, bias, vec, aid, pic)
    if group == 1:
        kv, off = qkv, 1
    else:
        kv = lax.all_gather(qkv[1:], "seq", axis=2, tiled=True, axis_index_groups=teams)
        off = 0
    probs, oaug, *got = attn_fwd_call(qkv, kv, off, second)
    if fast:
        weights, cot = got[:2], got[2].reshape(count, d)
    more = ((0, 0), (0, 0), (0, 0), (0, fslot - fs))
    ff = jnp.pad(jnp.swapaxes(wide.reshape(2, LORA, seq, fs), 1, 2), more)
    bup = jnp.pad(bup, more[1:])
    mixed, dmid, d_out, g_mid, *got = mid_call(
        oaug, x, cot, aid, wo, weights, cuts, jnp.concatenate([at[3:], b[3:]]), ff, bup, vec, last)

    def blocks(t):
        return t.reshape(2, 2, 2 * nz, 8, t.shape[2])

    third_comm = Settle(nz, blocks(g_mid), mixed.reshape(rows, part_len, d), 4) if fast else Quiet()
    dq, dk, dv, *got = attn_bwd_call(qkv, kv, off, probs, oaug, d_out, third_comm)
    if fast:
        g_mid, mixed = got[0].reshape(2, LORA // seq, -1), got[1]
    if group > 1:
        dk, dv = (lax.psum_scatter(t, "seq", scatter_dimension=1, axis_index_groups=teams, tiled=True)
                  for t in (dk, dv))
    d_in, d_low, g_qkv = tail_call(dq, dk, dv, x, n1, hid, dmid, aid, wq, wk, wv, at, bq, vec)
    if fast:
        g_qkv, other = finish_call(nz, blocks(g_qkv), d_low.reshape(rows, part_len, d))
        g_qkv = g_qkv.reshape(2, LORA // seq, -1)
        mine = lax.dynamic_index_in_dim(d_in.reshape(rows, part_len, d), me, 0, False)
        other = other.astype(f32)
        d_in = jnp.where(me == 0, jnp.stack([mine, other]), jnp.stack([other, mine]))
    else:
        def total(t):
            return lax.psum(lax.psum_scatter(t, "seq", scatter_dimension=1, tiled=True), "dp")

        g_mid, g_qkv = total(g_mid), total(g_qkv)
        mixed = from_row(mixed, bf16)
        d_in = from_row(d_in, f32)

    def down_form(t):
        return jnp.swapaxes(t.astype(f32).reshape(-1, RANK, t.shape[-1]), -1, -2)

    def up_form(t):
        return t.astype(f32).reshape(-1, RANK, t.shape[-1])

    def cut(t, k):
        return t[:, k * d:(k + 1) * d]

    def ff_of(t):
        return jnp.concatenate([t[:, 2 * d + j * fslot:2 * d + j * fslot + fs] for j in range(seq)], axis=1)

    a_mid, b_mid = g_mid
    a_qkv, b_qkv = g_qkv
    return (
        mixed,
        d_in,
        jnp.stack([down_form(cut(a_qkv, p)) for p in range(3)]),
        down_form(cut(a_mid, 0)),
        jnp.stack([up_form(cut(b_qkv, p)) for p in range(3)] + [up_form(cut(b_mid, 0))]),
        down_form(cut(a_mid, 1)),
        up_form(ff_of(b_mid)),
        down_form(ff_of(a_mid)),
        up_form(cut(b_mid, 1)),
    )


def solution(mesh):
    both = P("dp", "seq", None)
    lead = P("seq", None, None)
    second = P(None, "seq", None, None)
    return jax.shard_map(
        local,
        mesh=mesh,
        in_specs=(both, both, P("dp", None), P("dp", None))
        + (P("dp", "seq"),) * 5 + (P("seq", "dp"),) + (P("seq"),) * 9
        + (second, lead, second, lead, lead, lead, lead),
        out_specs=(both, both, second, lead, second, lead, lead, lead, lead),
        check_vma=False,
    )
```

profile of v0, /device:TPU:0, one launch (start us, length us, event | category | flops | bytes accessed | tf_op | source)
XLA Modules:
  0.0 572.2 jit_solution(15782890872665099516)
XLA Ops:
  9.4 1.6 pad_slice_fusion
  11.0 1.8 fusion.15
  13.0 1.5 fusion.refs_8_.refs_3_.aid_ref
  17.3 125.5 %front.1 = (bf16[32,40,1152]{2,1,0:T(8,128)(2,1)}, bf16[32,72,576]{2,1,0:T(8,128)(2,1)}, bf16[32,72,576]{2,1,0:T(8,128)(2,1)}, bf16[32,72,576]{2,1,0:T(8,128)(2,...) custom-call(bf16[40,1152]{1,0:T(8,128)(2,1)} %constant_dynamic-slice, ...), custom_call_target="tpu_custom_call" | custom-call | tf_op jit(solution)/shard_map/front/pallas_call | solution.py:500
  145.7 1.8 copy.54
  147.5 3.0 reshape_reshape.3
  150.5 1.9 copy.53
  152.4 1.6 pad.27.refs_6_
  153.9 1.1 copy-done.2
  156.3 3.5 reshape.158
  159.8 2.3 copy.55
  162.1 1.3 slice.142
  163.4 1.1 pad_maximum_fusion.refs_5_
  164.6 84.7 %attn_fwd.1 = (bf16[16,1024,1024]{2,1,0:T(8,128)(2,1)}, bf16[16,1024,128]{2,1,0:T(8,128)(2,1)}, bf16[32,72,768]{2,1,0:T(8,128)(2,1)}, bf16[32,72,768]{2,1,0:T(8,128)(2,1)}, bf16[2,512,1152]{2,1,0:T(8,128)(2,1)}) custom-call(bf16[3,16,1024,128]{3,2,1,0:T(8,128)(2,1)} %get-tuple-element.39.q_ref.k_ref.v_ref, ...), custom_call_target="tpu_custom_call" | custom-call | tf_op jit(solution)/shard_map/attn_fwd/pallas_call | solution.py:790
  249.3 147.7 %mid.1 = (bf16[1024,1152]{1,0:T(8,128)(2,1)}, f32[1024,1152]{1,0:T(8,128)}, bf16[16,1024,128]{2,1,0:T(8,128)(2,1)}, bf16[2,128,6656]{2,1,0:T(8,128)(2,1)}, bf16[...) custom-call(bf16[16,1024,128]{2,1,0:T(8,128)(2,1)} %get-tuple-elemen, ...), custom_call_target="tpu_custom_call" | custom-call | tf_op jit(solution)/shard_map/mid/pallas_call | solution.py:1042
  397.0 85.8 %attn_bwd.1 = (bf16[16,1024,128]{2,1,0:T(8,128)(2,1)}, bf16[16,1024,128]{2,1,0:T(8,128)(2,1)}, bf16[16,1024,128]{2,1,0:T(8,128)(2,1)}, bf16[2,8,8,6656]{3,2,1,0:T(8,128)(2,1)}, bf16[2,512,1152]{2,1,0:T(8,128)(2,1)}) custom-call(bf16[3,16,1024,128]{3,2,1,0:T(8,128)(2,1)} %get-tuple-element.39.q_ref.k_ref.v_ref, ...), custom_call_target="tpu_custom_call" | custom-call | tf_op jit(solution)/shard_map/attn_bwd/pallas_call | solution.py:837
  482.8 31.9 %tail.1 = (f32[1024,1152]{1,0:T(8,128)}, bf16[1024,1152]{1,0:T(8,128)(2,1)}, bf16[2,128,3456]{2,1,0:T(8,128)(2,1)}) custom-call(bf16[16,1024,128]{2,1,0:T(8,128)(2,1)} %get-tuple-element.54.dq_ref, bf16[16,1024,128]{2,1,0:T(8,128)(2,1)} %get-tuple-element.55.dk_ref, bf16[16,1024,128]{2,1,0:T(8,128)(2,1)} %get-tuple-element.56.dv_ref, ...), custom_call_target="tpu_custom_call" | custom-call | tf_op jit(solution)/shard_map/tail/pallas_call | solution.py:1112
  514.8 2.0 constant_dynamic-slice_fusion
  517.7 43.1 %finish.1 = (bf16[2,8,8,3456]{3,2,1,0:T(8,128)(2,1)S(1)}, bf16[512,1152]{1,0:T(8,128)(2,1)S(1)}) custom-call(bf16[2,2,8,8,3456]{4,3,2,1,0:T(8,128)(2,1)S(1)} %bitcast.110, bf16[2,512,1152]{2,1,0:T(8,128)(2,1)S(1)} %bitcast.109), custom_call_target="tpu_custom_call" | custom-call | tf_op jit(solution)/shard_map/finish/pallas_call | solution.py:539
  562.0 2.5 maximum_select_fusion
  567.0 1.2 convert_bitcast_fusion
  568.2 1.2 maximum_convert_fusion.1
  569.3 1.1 maximum_convert_fusion
  570.4 1.4 copy.61
  (71 shorter events, 20.4 us)
Async XLA Ops:
  0.6 15.0 %copy-start.7 = (bf16[4,4304,16]{1,2,0:T(8,128)(2,1)S(1)}, bf16[4,4304,16]{1,2,0:T(8,128)(2,1)}, u32[]{:S(2)}) copy-start(bf16[4,4304,16]{1,2,0:T(8,128)(2,1)} %param.50) | copy-start | bytes 1652740
  0.7 15.0 %copy-start.6 = (bf16[4,16,4304]{2,1,0:T(8,128)(2,1)S(1)}, bf16[4,16,4304]{2,1,0:T(8,128)(2,1)}, u32[]{:S(2)}) copy-start(bf16[4,16,4304]{2,1,0:T(8,128)(2,1)} %param.49) | copy-start | bytes 1652740
  12.8 3.6 copy-start.8
  13.0 3.4 copy-start.9
  14.6 1.9 copy-start.10
  14.6 1.9 copy-start.5
  15.6 1.0 copy-start.11
  152.4 2.6 copy-start.2
  514.8 2.4 copy-start
  514.8 2.9 copy-start.1
  562.0 2.5 copy-start.4
  567.0 3.4 copy-start.3
where the time goes:
time: 583 us; the launch traced here: 572 us
  Pallas kernels  519 us (89%)
  local copies, waits for them, and re-layouts  37.8 us (6%)
  other arithmetic  14.3 us (2%)
    pallas_call x1, Pallas kernels, mid_call(): pl.pallas_call(partial(mid_kernel, s, pieces, cuts, comm), in_specs=any_s...  148 us
    pallas_call x1, Pallas kernels, front_call(): pl.pallas_call(partial(front_kernel, nz, na), in_specs=any_specs(na + 2)...  126 us
    pallas_call x1, Pallas kernels, attn_bwd_call(): pl.pallas_call(partial(attn_bwd_kernel, tq, comm), grid=(HEADS,), in_spec...  85.8 us
    pallas_call x1, Pallas kernels, attn_fwd_call(): pl.pallas_call(partial(attn_fwd_kernel, tq, comm), grid=(HEADS,), in_spec...  84.7 us
    pallas_call x1, Pallas kernels, finish_call(): pl.pallas_call(partial(finish_kernel, nz), in_specs=[pl.BlockSpec(memory_...  43.1 us
    pallas_call x1, Pallas kernels, tail_call(): pl.pallas_call(partial(tail_kernel, s), grid=(tokens // tm,), in_specs=[h...  31.9 us

commit v1 on v0

--- a/solution.py
+++ b/solution.py
@@ -106,15 +106,13 @@
     def __init__(self, spot, parts, ins, outs, send, recv, core, own):
         self.s, self.parts, self.ins, self.outs = spot, parts, ins, outs
         self.send, self.recv, self.core, self.own = send, recv, core, own
-        self.slot = {}
-        for kind, r in self.kinds:
-            for to in self.targets(kind, r):
-                self.slot[kind, r, to] = len(self.slot)
+        every = [to for kind, r in self.kinds for to in self.targets(kind, r)]
+        self.counts = sum(to[0] != "i" for to in every), sum(to[0] == "i" for to in every)
 
     @staticmethod
     def scratch(nz, count):
         dma = pltpu.SemaphoreType.DMA
-        return [dma((count, 36)), dma((count, 4 * nz)), dma((count,)), dma((count,))]
+        return [dma((count, 2)), dma((count, 4 * nz)), dma((count,)), dma((count,))]
 
     def targets(self, kind, r):
         if kind == "z":
@@ -163,17 +161,8 @@
             else:
                 there = 1 if to == "z1" else 2
             recv, device = self.arrival(g, kind, there), s.zp[i]
-        send = self.send.at[g, self.slot[kind, r, to]]
+        send = self.send.at[g, int(to[0] == "i")]
         return remote(self.source(g, kind, r), self.place(g, self.index(kind, r)), send, recv, device)
-
-    def each(self, g, kind, r, act):
-        for to in self.targets(kind, r):
-            if to[0] == "i":
-                @pl.when(self.s.inner == 1)
-                def _(to=to):
-                    act(self.copy(g, kind, r, to))
-            else:
-                act(self.copy(g, kind, r, to))
 
     def local(self, g):
         return pltpu.make_async_copy(self.source(g, "z", 0), self.place(g, self.index("z", 0)), self.own.at[g])
@@ -184,18 +173,27 @@
         else:
             ref = self.place(g, self.index(kind, r))
             remote(ref, ref, self.send.at[g, 0], self.arrival(g, kind, r), self.s.xn).wait_recv()
-        self.each(g, kind, r, lambda copy: copy.start())
+        for to in self.targets(kind, r):
+            if to[0] == "i":
+                pl.when(self.s.inner == 1)(self.copy(g, kind, r, to).start)
+            else:
+                self.copy(g, kind, r, to).start()
+
+    def several(self, g, n, which=0):
+        a, start, size = self.parts[g]
+        ref = self.outs[a].at[pl.ds(0, n)]
+        if size < self.outs[a].shape[2]:
+            ref = self.outs[a].at[pl.ds(0, n), :, pl.ds(start, size)]
+        return remote(ref, ref, self.send.at[g, which], self.core.at[g], self.s.sib)
 
     def end(self, g):
-        a, start, size = self.parts[g]
-        n = self.outs[a].shape[0] // 2
-        ref = self.outs[a].at[pl.ds(0, n), :, pl.ds(start, size)]
-        if size == self.outs[a].shape[2]:
-            ref = self.outs[a].at[pl.ds(0, n)]
-        remote(ref, ref, self.send.at[g, 0], self.core.at[g], self.s.sib).wait_recv()
+        self.several(g, self.outs[self.parts[g][0]].shape[0] // 2).wait_recv()
         self.local(g).wait()
-        for kind, r in self.kinds:
-            self.each(g, kind, r, lambda copy: copy.wait_send())
+        self.several(g, self.counts[0]).wait_send()
+
+        @pl.when(self.s.inner == 1)
+        def _():
+            self.several(g, self.counts[1], 1).wait_send()
 
     def actions(self):
         n = len(self.parts)
@@ -379,139 +377,6 @@
         return [(f,) for f in (self.one, self.two, self.three, self.four, self.five, self.six, self.seven, self.end)]
 
 
-def front_kernel(nz, na, *refs):
-    shards, (tokens, vec, aid_ref, pic_ref), refs = refs[:na], refs[na:na + 4], refs[na + 4:]
-    wholes, (x_out, vec_out, qkv_out, n1_out, h_out), refs = refs[:na], refs[na:na + 5], refs[na + 5:]
-    (xbuf, vbuf, nbuf, wbuf, abuf, bbuf, n1, hbuf, heads, sems, wsem, osem, *refs) = refs
-    n, d = nz * 4, xbuf.shape[2]
-    count, tm = 2 * xbuf.shape[1], 512
-    ds = wbuf.shape[3]
-    nh = ds // HEAD_DIM
-    spot = Spot(nz)
-    spot.barrier()
-    gather = Gather(spot, [(k, 0, a.shape[1]) for k, a in enumerate(shards)], shards, wholes, *refs)
-    run = Steps(gather.actions())
-    vec_here = pltpu.make_async_copy(vec, vbuf.at[spot.x], sems.at[0])
-    vec_there = remote(vec, vbuf.at[spot.x], sems.at[1], sems.at[2], spot.xn)
-    row_here = pltpu.make_async_copy(tokens.at[spot.x], xbuf.at[spot.x], sems.at[3])
-    row_there = remote(tokens.at[1 - spot.x], xbuf.at[spot.x], sems.at[4], sems.at[5], spot.xn)
-    vec_here.start()
-    vec_there.start()
-    run.step(2)
-    row_here.start()
-    row_there.start()
-    run.step(13)
-
-    vec_here.wait()
-    got = vbuf.at[1 - spot.x]
-    remote(got, got, sems.at[1], sems.at[2], spot.xn).wait_recv()
-    row_here.wait()
-    got = xbuf.at[1 - spot.x]
-    remote(got, got, sems.at[4], sems.at[5], spot.xn).wait_recv()
-    gain, shift = (jnp.concatenate([vbuf[j, k:k + 1, :ds] for j in range(2)], axis=1).astype(f32) for k in (4, 5))
-    keep = [pltpu.make_async_copy(xbuf, x_out, osem.at[0]), pltpu.make_async_copy(vbuf, vec_out, osem.at[1])]
-    for copy in keep:
-        copy.start()
-    for half in range(2):
-        def norm_step(i, carry, half=half):
-            nhat, _ = norm_parts(xbuf[half, pl.ds(i * 256, 256), :].astype(f32))
-            n1[pl.ds(half * (count // 2) + i * 256, 256), :d] = (nhat * gain + shift).astype(bf16)
-            return carry
-        lax.fori_loop(0, count // 512, norm_step, 0)
-        run.step(4)
-    keep.append(pltpu.make_async_copy(n1.at[:, pl.ds(0, d)], n1_out, osem.at[2]))
-    keep[-1].start()
-
-    run.until(0)
-    small = pltpu.make_async_copy(wholes[0], nbuf, sems.at[6])
-    small.start()
-    small.wait()
-    each = LORA // 2
-    for m in range(3):
-        for j in range(2):
-            rows = slice(j * each, (j + 1) * each)
-            one = nbuf[j * n:(j + 1) * n].reshape(10 * each, d)
-            abuf[m, rows, :] = one[m * each:(m + 1) * each]
-            for i in range(2):
-                bbuf[m, i, rows, :] = one[(5 + m) * each:(6 + m) * each, i * ds:(i + 1) * ds]
-
-    def fetch(p, j):
-        return pltpu.make_async_copy(wholes[1 + p].at[pl.ds(j * n, n)], wbuf.at[j], wsem.at[j])
-
-    blocks = []
-    for p in range(3):
-        run.until(1 + p)
-        for j in range(2):
-            fetch(p, j).start()
-        for i in range(count // tm):
-            rows = pl.ds(i * tm, tm)
-            h = (nt(n1[rows, :d], abuf[p]) * column_mask(aid_ref[rows, :])).astype(bf16)
-            hbuf[p, rows, :] = h
-            n1[rows, d:] = (0.5 * h.astype(f32)).astype(bf16)
-        for j in range(2):
-            fetch(p, j).wait()
-            bias = vbuf[j, p // 2:p // 2 + 1, :ds].astype(f32) if p != 1 else 0.0
-
-            def step(i, carry, p=p, j=j, bias=bias):
-                rows = pl.ds(i * tm, tm)
-                run.within(i, 1, count // tm, 3)
-                w = jnp.concatenate([wbuf[j].reshape(d, ds), bbuf[p, j]])
-                y = (nn(n1[rows, :], w) + bias).astype(bf16)
-                place = lax.broadcasted_iota(jnp.int32, (tm, LANES), 1) - HEAD_DIM
-                same = place == pic_ref[rows, :]
-                if p == 0:
-                    extra = jnp.where(same, 1.0, 0.0)
-                elif p == 1:
-                    extra = jnp.where((place >= 0) & (place < 16) & jnp.logical_not(same), -BIG, 0.0)
-                else:
-                    extra = jnp.where((place == 0) | (place == 1), 1.0, 0.0)
-                extra = extra.astype(bf16)[:, HEAD_DIM:]
-                for h in range(nh):
-                    heads[p, j * nh + h, rows, :HEAD_DIM] = y[:, h * HEAD_DIM:(h + 1) * HEAD_DIM]
-                    heads[p, j * nh + h, rows, HEAD_DIM:] = extra
-                return carry
-            lax.fori_loop(0, count // tm, step, 0)
-            which = pl.ds(j * nh, nh)
-            blocks.append(pltpu.make_async_copy(heads.at[p, which], qkv_out.at[p, which], osem.at[4 + 2 * p + j]))
-            blocks[-1].start()
-            run.step(3)
-    keep.append(pltpu.make_async_copy(hbuf, h_out, osem.at[3]))
-    keep[-1].start()
-    run.rest()
-    for copy in keep + blocks:
-        copy.wait()
-    vec_there.wait_send()
-    row_there.wait_send()
-
-
-def front_call(nz, shards, tokens, vec, aid, pic):
-    na = len(shards)
-    dma = pltpu.SemaphoreType.DMA
-    count, d = 2 * tokens.shape[1], tokens.shape[2]
-    ds = shards[1].shape[1]
-    full = pl.BlockSpec(memory_space=pltpu.VMEM)
-
-    def v(*shape):
-        return pltpu.VMEM(shape, bf16)
-
-    def out(*shape):
-        return jax.ShapeDtypeStruct(shape, bf16)
-
-    return pl.pallas_call(
-        partial(front_kernel, nz, na),
-        in_specs=any_specs(na + 2) + [full, full],
-        out_specs=any_specs(na + 5),
-        out_shape=gathered(nz, shards) + [
-            out(*tokens.shape), out(2, *vec.shape), out(3, HEADS, count, LANES), out(count, d), out(3, count, LORA)],
-        scratch_shapes=[
-            v(*tokens.shape), v(2, *vec.shape), v(8 * nz, *shards[0].shape), v(2, 4 * nz, *shards[1].shape),
-            v(3, LORA, d), v(3, 2, LORA, ds), v(count, d + LORA), v(3, count, LORA), v(3, HEADS, count, LANES),
-            dma((7,)), dma((2,)), dma((10,))] + Gather.scratch(nz, na),
-        compiler_params=pltpu.CompilerParams(collective_id=1, has_side_effects=True, vmem_limit_bytes=VMEM),
-        name="front",
-    )(*shards, tokens, vec, aid, pic)
-
-
 def any_specs(n):
     return [pl.BlockSpec(memory_space=pl.ANY)] * n
 
@@ -552,10 +417,17 @@
     def __init__(self, actions):
         self.actions = list(actions)
 
+    def take(self, count):
+        out, self.actions = self.actions[:count], self.actions[count:]
+        return out
+
+    @staticmethod
+    def do(actions):
+        for action in actions:
+            action[0](*action[1:])
+
     def step(self, count):
-        for action in self.actions[:count]:
-            action[0](*action[1:])
-        del self.actions[:count]
+        self.do(self.take(count))
 
     def rest(self):
         self.step(len(self.actions))
@@ -565,9 +437,16 @@
         if ends:
             self.step(ends[0] + 1)
 
-    def within(self, i, first, last, count):
-        for t in range(first, last):
-            pl.when(i == t)(partial(self.step, count))
+    def within(self, first, last, *counts):
+        plan = [(t, [self.take(count) for count in counts]) for t in range(first, last)]
+
+        def point(k):
+            def run(i):
+                for t, lists in plan:
+                    if lists[k]:
+                        pl.when(i == t)(partial(self.do, lists[k]))
+            return run
+        return [point(k) for k in range(len(counts))]
 
 
 class Quiet:
@@ -871,14 +750,9 @@
     return g, dg
 
 
-def mid_kernel(s, n, cuts, comm, *refs):
-    own, refs = refs[:9 + 2 * comm.ready], refs[9 + 2 * comm.ready:]
-    oaug_ref, x_ref, cot_ref, aid_ref, wo_ref, ab_ref, ff_ref, bup_ref, vec_ref = own[:9]
-    weights = list(own[9:])
-    ins, (mixed_ref, dmid_ref, do_ref, pack_ref), outs, refs = comm.split(refs, 4)
-    (obuf, xbuf, dybuf, wobuf, ocat, n2buf, mid, acc, dn2, hidden, wofull, ubuf, dbuf, ga, gb, isem, wsem, osem,
-     go, cotbuf, lsem, *comm_refs) = refs
-    weights += list(outs[:2 * (len(cuts) - comm.ready)])
+def mid_work(s, n, cuts, run, ready, part, weights, load, save, wo_load, bufs):
+    (aid_ref, ab_ref, ff_ref, bup_ref, vec_ref, pack_ref, obuf, xbuf, cotbuf, dybuf, wobuf, ocat, n2buf, mid, acc, dn2,
+     hidden, wofull, ubuf, dbuf, ga, gb, wsem, go) = bufs
     tokens, d = xbuf.shape
     ds = d // s
     bo, bd, gain2, shift2 = vec_ref[2:3, :], vec_ref[3:4, :], vec_ref[6:7, :], vec_ref[7:8, :]
@@ -886,19 +760,6 @@
     ta, tm = min(256, tokens), min(512, tokens)
     chunks = [(c, j) for c in range(len(cuts)) for j in range(s)]
 
-    def load(i):
-        rows = pl.ds(i * ta, ta)
-        for k, (src, dst) in enumerate(((oaug_ref.at[:, rows], obuf.at[:, rows]), (x_ref.at[rows], xbuf.at[rows]),
-                                        (cot_ref.at[rows], cotbuf.at[rows]))):
-            yield pltpu.make_async_copy(src, dst, isem.at[i, k])
-
-    def save(i):
-        rows = pl.ds(i * ta, ta)
-        for k, (src, dst) in enumerate(((xbuf.at[rows], mixed_ref.at[rows]), (mid.at[rows], dmid_ref.at[rows]),
-                                        (obuf.at[:, rows], do_ref.at[:, rows]))):
-            yield pltpu.make_async_copy(src, dst, osem.at[i, k])
-
-    wo_load = pltpu.make_async_copy(wo_ref, wobuf, lsem.at[0])
     def fetch(k):
         c, j = chunks[k]
         w = cuts[c][1]
@@ -906,22 +767,25 @@
             dst = buf.at[k % 2] if w == buf.shape[3] else buf.at[k % 2, :, :, pl.ds(0, w)]
             yield pltpu.make_async_copy(ref.at[pl.ds(j * n, n)], dst, wsem.at[k % 2, m])
 
-    wo_load.start()
+    for copy in wo_load:
+        copy.start()
     for i in range(tokens // ta):
         for copy in load(i):
             copy.start()
-    run = comm.begin(ins, outs, comm_refs)
-    for copy in fetch(0):
-        copy.start()
-    wo_load.wait()
+    if ready:
+        for copy in fetch(0):
+            copy.start()
+    for copy in wo_load:
+        copy.wait()
     run.step(4)
 
-    wo = jnp.concatenate([wobuf[j][:, :ds] for j in range(s)], axis=1) if s > 1 else wobuf[0]
-    wofull[...] = wo
+    wofull[...] = jnp.concatenate([wobuf[j].reshape(d, ds) for j in range(s)], axis=1)
+
+    [serve] = run.within(1, tokens // ta, 3)
 
     def before(i, carry):
         rows = pl.ds(i * ta, ta)
-        run.within(i, 1, tokens // ta, 4)
+        serve(i)
         for copy in load(i):
             copy.wait()
         mask = column_mask(aid_ref[rows, :])
@@ -944,7 +808,11 @@
 
     for k, (c, j) in enumerate(chunks):
         start, w = cuts[c]
-        late = k + 1 < len(chunks) and chunks[k + 1][0] >= comm.ready and chunks[k + 1][1] == 0
+        if k == 0 and not ready:
+            run.until(part(0))
+            for copy in fetch(0):
+                copy.start()
+        late = k + 1 < len(chunks) and chunks[k + 1][0] >= ready and chunks[k + 1][1] == 0
         if k + 1 < len(chunks) and not late:
             for copy in fetch(k + 1):
                 copy.start()
@@ -952,9 +820,11 @@
             copy.wait()
         cols = slice(start, start + w)
 
-        def chunk(i, carry, k=k, j=j, w=w, cols=cols, slot=k % 2):
+        [serve] = run.within(1, tokens // tm, 8)
+
+        def chunk(i, carry, k=k, j=j, w=w, cols=cols, slot=k % 2, serve=serve):
             rows = pl.ds(i * tm, tm)
-            run.within(i, 1, tokens // tm, 8)
+            serve(i)
             wu = jnp.concatenate([ubuf[slot, :, :, :w].reshape(d, w), ff_ref[1, j, :, cols]])
             wd = jnp.concatenate([dbuf[slot, :, :, :w].reshape(d, w), ff_ref[0, j, :, cols]])
             z = nn(n2buf[rows, :], wu) + bup_ref[j, :, cols]
@@ -986,7 +856,7 @@
         pack_ref[1, :, at:at + w] = gb[:, :w].astype(bf16)
         run.step(8)
         if late:
-            run.until(2 * (chunks[k + 1][0] - comm.ready) + 1)
+            run.until(part(chunks[k + 1][0]))
             for copy in fetch(k + 1):
                 copy.start()
 
@@ -1025,40 +895,286 @@
             copy.wait()
 
 
-def mid_call(oaug, x, cot, aid, wo, weights, cuts, ab, ff, bup, vec, comm):
+def mid_kernel(s, n, cuts, *refs):
+    (oaug_ref, x_ref, cot_ref, aid_ref, wo_ref, ab_ref, ff_ref, bup_ref, vec_ref) = refs[:9]
+    weights, refs = refs[9:9 + 2 * len(cuts)], refs[9 + 2 * len(cuts):]
+    mixed_ref, dmid_ref, do_ref, pack_ref, obuf, xbuf, isem, osem, lsem, *bufs = refs
+    cotbuf, mid = bufs[0], bufs[5]
+    ta = min(256, xbuf.shape[0])
+
+    def load(i):
+        rows = pl.ds(i * ta, ta)
+        for k, (src, dst) in enumerate(((oaug_ref.at[:, rows], obuf.at[:, rows]), (x_ref.at[rows], xbuf.at[rows]),
+                                        (cot_ref.at[rows], cotbuf.at[rows]))):
+            yield pltpu.make_async_copy(src, dst, isem.at[i, k])
+
+    def save(i):
+        rows = pl.ds(i * ta, ta)
+        for k, (src, dst) in enumerate(((xbuf.at[rows], mixed_ref.at[rows]), (mid.at[rows], dmid_ref.at[rows]),
+                                        (obuf.at[:, rows], do_ref.at[:, rows]))):
+            yield pltpu.make_async_copy(src, dst, osem.at[i, k])
+
+    mid_work(s, n, cuts, Steps([]), len(cuts), None, weights, load, save,
+             [pltpu.make_async_copy(wo_ref, bufs[2], lsem.at[0])],
+             [aid_ref, ab_ref, ff_ref, bup_ref, vec_ref, pack_ref, obuf, xbuf] + bufs)
+
+
+def mid_bufs(s, pieces, tokens, d, widest):
+    def v(*shape, dtype=bf16):
+        return pltpu.VMEM(shape, dtype)
+
+    return [
+        v(tokens, d), v(tokens, d + LORA), v(s, d, d // s), v(tokens, d), v(tokens, d + LORA),
+        v(tokens, d, dtype=f32), v(tokens, d + LORA, dtype=f32), v(tokens, d + LORA, dtype=f32),
+        v(tokens, LORA), v(d, d), v(2, pieces, d // pieces, widest), v(2, pieces, d // pieces, widest),
+        v(LORA, widest, dtype=f32), v(LORA, widest, dtype=f32), pltpu.SemaphoreType.DMA((2, 2)),
+        v(4, LORA, d, dtype=f32),
+    ]
+
+
+def mid_call(oaug, x, cot, aid, wo, weights, cuts, ab, ff, bup, vec):
     tokens, d = x.shape
-    s, ds = wo.shape[0], wo.shape[2]
+    s = wo.shape[0]
     pieces = weights[0].shape[0] // s
-    widest = max(w for _, w in cuts)
-    fslot = ff.shape[3]
+    tiles = tokens // min(256, tokens)
     full = pl.BlockSpec(memory_space=pltpu.VMEM)
     dma = pltpu.SemaphoreType.DMA
-    comm.ready = len(weights) // 2
-    tiles = tokens // min(256, tokens)
-
-    def v(*shape, dtype=bf16):
-        return pltpu.VMEM(shape, dtype)
-
     return pl.pallas_call(
-        partial(mid_kernel, s, pieces, cuts, comm),
-        in_specs=any_specs(3) + [full] + any_specs(1) + [full] * 4 + any_specs(len(weights)) + comm.in_specs(),
-        out_specs=any_specs(3) + [full] + comm.out_specs(),
+        partial(mid_kernel, s, pieces, cuts),
+        in_specs=any_specs(3) + [full] + any_specs(1) + [full] * 4 + any_specs(len(weights)),
+        out_specs=any_specs(3) + [full],
         out_shape=[
             jax.ShapeDtypeStruct((tokens, d), bf16),
             jax.ShapeDtypeStruct((tokens, d), f32),
             jax.ShapeDtypeStruct((HEADS, tokens, LANES), bf16),
-            jax.ShapeDtypeStruct((2, LORA, 2 * d + s * fslot), bf16),
-        ] + comm.out_shape(),
+            jax.ShapeDtypeStruct((2, LORA, 2 * d + s * ff.shape[3]), bf16),
+        ],
         scratch_shapes=[
-            v(HEADS, tokens, LANES), v(tokens, d), v(tokens, d + LORA), v(s, d, ds), v(tokens, d), v(tokens, d + LORA),
-            v(tokens, d, dtype=f32), v(tokens, d + LORA, dtype=f32), v(tokens, d + LORA, dtype=f32),
-            v(tokens, LORA), v(d, d), v(2, pieces, d // pieces, widest), v(2, pieces, d // pieces, widest),
-            v(LORA, widest, dtype=f32), v(LORA, widest, dtype=f32),
-            dma((tiles, 3)), dma((2, 2)), dma((tiles, 3)), v(4, LORA, d, dtype=f32), v(tokens, d), dma((1,)),
-        ] + comm.scratch(),
-        compiler_params=comm.params(),
+            pltpu.VMEM((HEADS, tokens, LANES), bf16), pltpu.VMEM((tokens, d), bf16),
+            dma((tiles, 3)), dma((tiles, 3)), dma((1,)),
+        ] + mid_bufs(s, pieces, tokens, d, max(w for _, w in cuts)),
+        compiler_params=pltpu.CompilerParams(vmem_limit_bytes=VMEM),
         name="mid",
-    )(oaug, x, cot, aid, wo, ab, ff, bup, vec, *weights, *comm.args)
+    )(oaug, x, cot, aid, wo, ab, ff, bup, vec, *weights)
+
+
+def forward_kernel(nz, cuts, na, *refs):
+    shards, (tokens, vec, cot, aid_ref, pic_ref), refs = refs[:na], refs[na:na + 5], refs[na + 5:]
+    wholes, refs = refs[:na], refs[na:]
+    (x_out, vec_out, qkv_out, n1_out, h_out, probs_out, o_out, cot_row, mixed_ref, dmid_ref, do_ref, pack_ref), refs = (
+        refs[:12], refs[12:])
+    (xbuf, vbuf, obuf, ab, ff, vecs, bups, sems, wsem, osem, psem, csems, isem, ssem, *gather_refs) = refs
+    n, d = nz * 4, xbuf.shape[2]
+    half = xbuf.shape[1]
+    count, tm = 2 * half, 512
+    ds, fslot = shards[1].shape[1], ff.shape[3]
+    nh = ds // HEAD_DIM
+    each = LORA // 2
+    spot = Spot(nz)
+    spot.barrier()
+    gather = Gather(spot, [(k, 0, a.shape[1]) for k, a in enumerate(shards)], shards, wholes, *gather_refs)
+    run = Steps(gather.actions())
+    swap = Swap(spot, cot, cot_row, csems)
+    vec_here = pltpu.make_async_copy(vec, vbuf.at[spot.x], sems.at[0])
+    vec_there = remote(vec, vbuf.at[spot.x], sems.at[1], sems.at[2], spot.xn)
+    row_here = pltpu.make_async_copy(tokens.at[spot.x], xbuf.at[spot.x], sems.at[3])
+    row_there = remote(tokens.at[1 - spot.x], xbuf.at[spot.x], sems.at[4], sems.at[5], spot.xn)
+
+    def first(nbuf, widebuf, wbuf, abuf, bbuf, n1, hbuf, heads, pbuf):
+        vec_here.start()
+        vec_there.start()
+        run.step(2)
+        row_here.start()
+        row_there.start()
+        run.step(13)
+        vec_here.wait()
+        got = vbuf.at[1 - spot.x]
+        remote(got, got, sems.at[1], sems.at[2], spot.xn).wait_recv()
+        row_here.wait()
+        got = xbuf.at[1 - spot.x]
+        remote(got, got, sems.at[4], sems.at[5], spot.xn).wait_recv()
+        for j in range(2):
+            vecs[:, j * ds:(j + 1) * ds] = vbuf[j, :8, :ds].astype(f32)
+            bups[j] = vbuf[j, 8:9, :].astype(f32)
+        gain, shift = vecs[4:5, :], vecs[5:6, :]
+        keep = [pltpu.make_async_copy(xbuf, x_out, osem.at[0]), pltpu.make_async_copy(vbuf, vec_out, osem.at[1])]
+        for copy in keep:
+            copy.start()
+        for part in range(2):
+            def norm_step(i, carry, part=part):
+                nhat, _ = norm_parts(xbuf[part, pl.ds(i * 256, 256), :].astype(f32))
+                n1[pl.ds(part * half + i * 256, 256), :d] = (nhat * gain + shift).astype(bf16)
+                return carry
+            lax.fori_loop(0, half // 256, norm_step, 0)
+            run.step(4)
+        keep.append(pltpu.make_async_copy(n1.at[:, pl.ds(0, d)], n1_out, osem.at[2]))
+        keep[-1].start()
+
+        run.until(0)
+        small = pltpu.make_async_copy(wholes[0], nbuf, sems.at[6])
+        small.start()
+        small.wait()
+        for j in range(2):
+            rows = slice(j * each, (j + 1) * each)
+            one = nbuf[j * n:(j + 1) * n].reshape(10 * each, d)
+            for m in range(3):
+                abuf[m, rows, :] = one[m * each:(m + 1) * each]
+                for i in range(2):
+                    bbuf[m, i, rows, :] = one[(5 + m) * each:(6 + m) * each, i * ds:(i + 1) * ds]
+            for k, m in enumerate((3, 4, 8, 9)):
+                ab[k, rows, :] = one[m * each:(m + 1) * each]
+
+        def fetch(p, j):
+            return pltpu.make_async_copy(wholes[1 + p].at[pl.ds(j * n, n)], wbuf.at[j], wsem.at[j])
+
+        for p in range(3):
+            run.until(1 + p)
+            for j in range(2):
+                fetch(p, j).start()
+            for i in range(count // tm):
+                rows = pl.ds(i * tm, tm)
+                h = (nt(n1[rows, :d], abuf[p]) * column_mask(aid_ref[rows, :])).astype(bf16)
+                hbuf[p, rows, :] = h
+                n1[rows, d:] = (0.5 * h.astype(f32)).astype(bf16)
+            for j in range(2):
+                fetch(p, j).wait()
+                bias = vbuf[j, p // 2:p // 2 + 1, :ds].astype(f32) if p != 1 else 0.0
+
+                [serve] = run.within(1, count // tm, 3)
+
+                def step(i, carry, p=p, j=j, bias=bias, serve=serve):
+                    rows = pl.ds(i * tm, tm)
+                    serve(i)
+                    w = jnp.concatenate([wbuf[j].reshape(d, ds), bbuf[p, j]])
+                    y = (nn(n1[rows, :], w) + bias).astype(bf16)
+                    place = lax.broadcasted_iota(jnp.int32, (tm, LANES), 1) - HEAD_DIM
+                    same = place == pic_ref[rows, :]
+                    if p == 0:
+                        extra = jnp.where(same, 1.0, 0.0)
+                    elif p == 1:
+                        extra = jnp.where((place >= 0) & (place < 16) & jnp.logical_not(same), -BIG, 0.0)
+                    else:
+                        extra = jnp.where((place == 0) | (place == 1), 1.0, 0.0)
+                    extra = extra.astype(bf16)[:, HEAD_DIM:]
+                    for h in range(nh):
+                        heads[p, j * nh + h, rows, :HEAD_DIM] = y[:, h * HEAD_DIM:(h + 1) * HEAD_DIM]
+                        heads[p, j * nh + h, rows, HEAD_DIM:] = extra
+                    return carry
+                lax.fori_loop(0, count // tm, step, 0)
+                which = pl.ds(j * nh, nh)
+                keep.append(pltpu.make_async_copy(
+                    heads.at[p, which], qkv_out.at[p, which], osem.at[4 + 2 * p + j]))
+                keep[-1].start()
+                run.step(3)
+        keep.append(pltpu.make_async_copy(hbuf, h_out, osem.at[3]))
+        keep[-1].start()
+        swap.start()
+
+        def probs_copy(h):
+            return pltpu.make_async_copy(pbuf.at[h % 2], probs_out.at[h], psem.at[h % 2])
+
+        serve, again = run.within(0, HEADS, 2, 1)
+
+        def head(h, carry):
+            serve(h)
+
+            @pl.when(h >= 2)
+            def _():
+                probs_copy(h - 2).wait()
+            for i in range(count // tm):
+                rows = pl.ds(i * tm, tm)
+                s = nt(heads[0, h, rows, :], heads[1, h])
+                top = jnp.max(s, axis=-1, keepdims=True)
+                p = jnp.exp2((s - top) * (SCALE * LOG2E)).astype(bf16)
+                o = nn(p, heads[2, h])
+                inv = 1.0 / o[:, HEAD_DIM:HEAD_DIM + 1]
+                pbuf[h % 2, rows, :] = (p.astype(f32) * inv).astype(bf16)
+                obuf[h, rows, :] = (o * inv).astype(bf16)
+            again(h)
+            probs_copy(h).start()
+            return carry
+        lax.fori_loop(0, HEADS, head, 0)
+        keep.append(pltpu.make_async_copy(obuf, o_out, osem.at[10]))
+        keep[-1].start()
+        run.until(5)
+        big = pltpu.make_async_copy(wholes[5], widebuf, sems.at[7])
+        big.start()
+        big.wait()
+        for j in range(2):
+            one = widebuf[j * n:(j + 1) * n].reshape(LORA, 2 * fslot)
+            for m in range(2):
+                for i in range(2):
+                    ff[m, i, j * each:(j + 1) * each, :] = one[m * each:(m + 1) * each, i * fslot:(i + 1) * fslot]
+        for h in range(HEADS - 2, HEADS):
+            probs_copy(h).wait()
+        for copy in keep:
+            copy.wait()
+
+    def v(*shape):
+        return pltpu.VMEM(shape, bf16)
+
+    pl.run_scoped(
+        first, v(8 * nz, *shards[0].shape), v(8 * nz, *shards[5].shape), v(2, n, *shards[1].shape), v(3, LORA, d),
+        v(3, 2, LORA, ds), v(count, d + LORA), v(3, count, LORA), v(3, HEADS, count, LANES), v(2, count, count))
+    swap.end()
+
+    def second(wobuf3, *bufs):
+        cotbuf, mid = bufs[0], bufs[4]
+        bufs = bufs[:2] + (wobuf3,) + bufs[2:]
+
+        def load(i):
+            yield pltpu.make_async_copy(cot_row.at[i * 256 // half, pl.ds(i * 256 % half, 256)],
+                                        cotbuf.at[pl.ds(i * 256, 256)], isem.at[i, 0])
+
+        def save(i):
+            rows = pl.ds(i * 256, 256)
+            inner = pl.ds(i * 256 % half, 256)
+            for k, (src, dst) in enumerate((
+                    (xrow.at[rows], mixed_ref.at[i * 256 // half, inner]), (mid.at[rows], dmid_ref.at[rows]),
+                    (obuf.at[:, rows], do_ref.at[:, rows]))):
+                yield pltpu.make_async_copy(src, dst, ssem.at[i, k])
+
+        mid_work(2, n, cuts, run, 0, lambda c: 7 + 2 * c, wholes[6:], load, save,
+                 [pltpu.make_async_copy(wholes[4].at[pl.ds(j * n, n)], wobuf3.at[j], isem.at[j, 1]) for j in range(2)],
+                 [aid_ref, ab, ff, bups, vecs, pack_ref, obuf, xrow] + list(bufs))
+
+    xrow = xbuf.reshape(count, d)
+    bufs = mid_bufs(2, n, count, d, max(w for _, w in cuts))
+    bufs[2] = v(2, n, d // n, ds)
+    pl.run_scoped(second, bufs[2], *bufs[:2], *bufs[3:])
+    vec_there.wait_send()
+    row_there.wait_send()
+
+
+def forward_call(nz, cuts, shards, tokens, vec, cot, aid, pic):
+    na = len(shards)
+    dma = pltpu.SemaphoreType.DMA
+    half, d = tokens.shape[1], tokens.shape[2]
+    count, fslot = 2 * half, shards[5].shape[1] // 2
+    tiles = count // 256
+    full = pl.BlockSpec(memory_space=pltpu.VMEM)
+
+    def v(*shape, dtype=bf16):
+        return pltpu.VMEM(shape, dtype)
+
+    def out(*shape, dtype=bf16):
+        return jax.ShapeDtypeStruct(shape, dtype)
+
+    return pl.pallas_call(
+        partial(forward_kernel, nz, cuts, na),
+        in_specs=any_specs(na + 3) + [full, full],
+        out_specs=any_specs(na + 11) + [full],
+        out_shape=gathered(nz, shards) + [
+            out(*tokens.shape), out(2, *vec.shape), out(3, HEADS, count, LANES), out(count, d), out(3, count, LORA),
+            out(HEADS, count, count), out(HEADS, count, LANES), out(*tokens.shape), out(*tokens.shape),
+            out(count, d, dtype=f32), out(HEADS, count, LANES), out(2, LORA, 2 * d + 2 * fslot)],
+        scratch_shapes=[
+            v(*tokens.shape), v(2, *vec.shape), v(HEADS, count, LANES), v(4, LORA, d), v(2, 2, LORA, fslot),
+            v(8, d, dtype=f32), v(2, 1, fslot, dtype=f32), dma((8,)), dma((2,)), dma((11,)), dma((2,)), dma((3,)),
+            dma((tiles, 2)), dma((tiles, 3))] + Gather.scratch(nz, na),
+        compiler_params=pltpu.CompilerParams(collective_id=1, has_side_effects=True, vmem_limit_bytes=VMEM),
+        name="forward",
+    )(*shards, tokens, vec, cot, aid, pic)
 
 
 def tail_kernel(s, dq_ref, dk_ref, dv_ref, x_ref, n1_ref, h_ref, dmid_ref, aid_ref,
@@ -1219,20 +1335,16 @@
             return t.reshape(seq, d, t.shape[2])
 
         small = jnp.concatenate([wide_to(vec_part, fslot), wide_to(b_up[None], fslot), jnp.zeros((7, fslot), bf16)])
-        narrow, wq, wk, wv, wo, wide, x, small, qkv, n1, hid = front_call(
-            nz, [share(narrow), w_query, w_key, w_value, w_out, share(wide)], tokens, small, aid, pic)
+        wide = jnp.pad(wide.reshape(2, -1, seq, fs), ((0, 0), (0, 0), (0, 0), (0, fslot - fs)))
+        wide = wide.reshape(2, -1, seq * fslot)
+        narrow, wq, wk, wv, *got = forward_call(
+            nz, cuts, [share(narrow), w_query, w_key, w_value, w_out, share(wide)] + ff_parts,
+            tokens, small, cotangent, aid, pic)
+        x, small, qkv, n1, hid, probs, oaug, _, mixed, dmid, d_out, g_mid = got[2 + len(ff_parts):]
         x = x.reshape(count, d)
         narrow = from_halves(narrow.reshape(seq, 10, LORA // seq, d))
         vec = jnp.concatenate([small[k, :8, :ds] for k in range(seq)], axis=1).astype(f32)
-        bup = small[:, 8:9, :fs].astype(f32)
-        wq, wk, wv, wo = whole(wq), whole(wk), whole(wv), whole(wo)
-        wide = from_halves(wide.reshape(seq, 2, LORA // seq, -1))
-
-        def fetch(shards, cid, halves=None):
-            return Fetch(nz, shards, [(k, 0, t.shape[1]) for k, t in enumerate(shards)], cid, halves)
-
-        second = fetch(ff_parts[:2], 3, cotangent)
-        last = fetch(ff_parts[2:], 6)
+        wq, wk, wv = whole(wq), whole(wk), whole(wv)
     else:
         def gather_all(shard):
             full = lax.all_gather(shard, ("seq", "dp"), axis=0, tiled=True)
@@ -1245,32 +1357,29 @@
         bup = lax.all_gather(b_up[None], "seq", axis=0, tiled=True).astype(f32)[:, None]
         x = to_row(tokens)
         cot = to_row(cotangent)
-        second = last = Quiet()
 
     at, b = narrow[:5], narrow[5:]
     bq = jnp.swapaxes(b[:3].reshape(3, LORA, seq, ds), 1, 2)
-    bias = jnp.stack([vec[0], jnp.zeros_like(vec[0]), vec[1]]).reshape(3, seq, 1, ds)
+    if group == 1:
+        off = 1
     if not fast:
-        wqkv = jnp.stack([wq, wk, wv])
-        qkv, n1, hid = qkv_call(x, wqkv, at, bq, bias, vec, aid, pic)
-    if group == 1:
-        kv, off = qkv, 1
-    else:
+        bias = jnp.stack([vec[0], jnp.zeros_like(vec[0]), vec[1]]).reshape(3, seq, 1, ds)
+        qkv, n1, hid = qkv_call(x, jnp.stack([wq, wk, wv]), at, bq, bias, vec, aid, pic)
+    kv = qkv
+    if group > 1:
         kv = lax.all_gather(qkv[1:], "seq", axis=2, tiled=True, axis_index_groups=teams)
         off = 0
-    probs, oaug, *got = attn_fwd_call(qkv, kv, off, second)
-    if fast:
-        weights, cot = got[:2], got[2].reshape(count, d)
-    more = ((0, 0), (0, 0), (0, 0), (0, fslot - fs))
-    ff = jnp.pad(jnp.swapaxes(wide.reshape(2, LORA, seq, fs), 1, 2), more)
-    bup = jnp.pad(bup, more[1:])
-    mixed, dmid, d_out, g_mid, *got = mid_call(
-        oaug, x, cot, aid, wo, weights, cuts, jnp.concatenate([at[3:], b[3:]]), ff, bup, vec, last)
+    if not fast:
+        probs, oaug = attn_fwd_call(qkv, kv, off, Quiet())
+        more = ((0, 0), (0, 0), (0, 0), (0, fslot - fs))
+        ff = jnp.pad(jnp.swapaxes(wide.reshape(2, LORA, seq, fs), 1, 2), more)
+        mixed, dmid, d_out, g_mid = mid_call(
+            oaug, x, cot, aid, wo, weights, cuts, jnp.concatenate([at[3:], b[3:]]), ff, jnp.pad(bup, more[1:]), vec)
 
     def blocks(t):
         return t.reshape(2, 2, 2 * nz, 8, t.shape[2])
 
-    third_comm = Settle(nz, blocks(g_mid), mixed.reshape(rows, part_len, d), 4) if fast else Quiet()
+    third_comm = Settle(nz, blocks(g_mid), mixed, 4) if fast else Quiet()
     dq, dk, dv, *got = attn_bwd_call(qkv, kv, off, probs, oaug, d_out, third_comm)
     if fast:
         g_mid, mixed = got[0].reshape(2, LORA // seq, -1), got[1]

time: 583 us -> 511 us (0.88)
  Pallas kernels: 519 us -> 461 us
  local copies, waits for them, and re-layouts: 37.8 us -> 25.6 us
    pallas_call x3 -> x1, Pallas kernels: 358 us -> 299 us  [forward_call(): pl.pallas_call(partial(forward_kernel, nz, cuts, na), in_specs=any_specs(...]
where the time goes in v1:
time: 511 us; the launch traced here: 501 us
  Pallas kernels  461 us (90%)
  local copies, waits for them, and re-layouts  25.6 us (5%)
  other arithmetic  13.6 us (3%)
    pallas_call x1, Pallas kernels, forward_call(): pl.pallas_call(partial(forward_kernel, nz, cuts, na), in_specs=any_specs(...  299 us
    pallas_call x1, Pallas kernels, attn_bwd_call(): pl.pallas_call(partial(attn_bwd_kernel, tq, comm), grid=(HEADS,), in_spec...  87 us
    pallas_call x1, Pallas kernels, finish_call(): pl.pallas_call(partial(finish_kernel, nz), in_specs=[pl.BlockSpec(memory_...  42.7 us
    pallas_call x1, Pallas kernels, tail_call(): pl.pallas_call(partial(tail_kernel, s), grid=(tokens // tm,), in_specs=[h...  31.9 us

profile of v1, /device:TPU:0, one launch (start us, length us, event | category | flops | bytes accessed | tf_op | source)
XLA Modules:
  0.0 501.3 jit_solution(8873637880948410503)
XLA Ops:
  0.7 0.8 fusion.9
  9.3 1.6 pad_slice_fusion
  11.0 1.9 fusion.17
  13.1 1.5 fusion.3.refs_15_.aid_ref
  14.6 1.0 copy.41.refs_16_
  16.4 1.1 fusion.2
  19.5 299.2 %forward.1 = (bf16[32,40,1152]{2,1,0:T(8,128)(2,1)}, bf16[32,72,576]{2,1,0:T(8,128)(2,1)}, bf16[32,72,576]{2,1,0:T(8,128)(2,1)}, bf16[32,72,576]{2,1,0:T(8,128)(...) custom-call(bf16[40,1152]{1,0:T(8,128)(2,1)} %constant_dynamic-slice, ...), custom_call_target="tpu_custom_call" | custom-call | tf_op jit(solution)/shard_map/forward/pallas_call | solution.py:1163
  318.6 87.0 %attn_bwd.1 = (bf16[16,1024,128]{2,1,0:T(8,128)(2,1)}, bf16[16,1024,128]{2,1,0:T(8,128)(2,1)}, bf16[16,1024,128]{2,1,0:T(8,128)(2,1)}, bf16[2,8,8,6656]{3,2,1,0:T(8,128)(2,1)}, bf16[2,512,1152]{2,1,0:T(8,128)(2,1)}) custom-call(bf16[3,16,1024,128]{3,2,1,0:T(8,128)(2,1)} %get-tuple-element.34.q_ref.k_ref.v_ref, ...), custom_call_target="tpu_custom_call" | custom-call | tf_op jit(solution)/shard_map/attn_bwd/pallas_call | solution.py:716
  407.1 1.5 slice_bitcast_fusion
  408.7 0.7 convert.25
  409.5 0.7 convert_bitcast_fusion.2
  410.3 0.7 convert_bitcast_fusion.1
  411.0 1.2 convert_bitcast_fusion
  412.2 1.2 maximum_convert_fusion.1
  413.7 1.3 slice.118
  415.0 0.9 reshape.141
  415.9 1.1 copy.48
  417.0 31.9 %tail.1 = (f32[1024,1152]{1,0:T(8,128)}, bf16[1024,1152]{1,0:T(8,128)(2,1)}, bf16[2,128,3456]{2,1,0:T(8,128)(2,1)}) custom-call(bf16[16,1024,128]{2,1,0:T(8,128)(2,1)} %get-tuple-element.41.dq_ref, bf16[16,1024,128]{2,1,0:T(8,128)(2,1)} %get-tuple-element.42.dk_ref, bf16[16,1024,128]{2,1,0:T(8,128)(2,1)} %get-tuple-element.43.dv_ref, ...), custom_call_target="tpu_custom_call" | custom-call | tf_op jit(solution)/shard_map/tail/pallas_call | solution.py:1228
  448.9 2.0 constant_dynamic-slice_fusion
  451.8 42.7 %finish.1 = (bf16[2,8,8,3456]{3,2,1,0:T(8,128)(2,1)S(1)}, bf16[512,1152]{1,0:T(8,128)(2,1)S(1)}) custom-call(bf16[2,2,8,8,3456]{4,3,2,1,0:T(8,128)(2,1)S(1)} %bitcast.95, bf16[2,512,1152]{2,1,0:T(8,128)(2,1)S(1)} %bitcast.94), custom_call_target="tpu_custom_call" | custom-call | tf_op jit(solution)/shard_map/finish/pallas_call | solution.py:404
  494.6 1.0 maximum_convert_fusion.2
  495.6 1.1 maximum_convert_fusion
  496.9 2.5 maximum_select_fusion
  499.5 1.4 copy.54
  (62 shorter events, 14.0 us)
Async XLA Ops:
  0.6 15.0 %copy-start.5 = (bf16[4,16,4304]{2,1,0:T(8,128)(2,1)S(1)}, bf16[4,16,4304]{2,1,0:T(8,128)(2,1)}, u32[]{:S(2)}) copy-start(bf16[4,16,4304]{2,1,0:T(8,128)(2,1)} %param.49) | copy-start | bytes 1652740
  11.0 5.0 %copy-start.6 = (bf16[4,4304,16]{1,2,0:T(8,128)(2,1)S(1)}, bf16[4,4304,16]{1,2,0:T(8,128)(2,1)}, u32[]{:S(2)}) copy-start(bf16[4,4304,16]{1,2,0:T(8,128)(2,1)} %param.50) | copy-start | bytes 1652740
  16.4 1.9 copy-start.7
  16.4 2.0 copy-start.8
  17.5 0.9 copy-start.9
  17.5 1.2 copy-start.4
  17.5 1.2 copy-start.10
  409.5 3.8 copy-start.2
  448.9 2.4 copy-start
  448.9 2.9 copy-start.1
  496.8 2.6 copy-start.3
